TPU v7x, 128 devices: a whole 4x4x4 slice. The times are simulated.
128 devices in a mesh: shard: 128 (over x, z, y, core).
Axes of the slice: x: 4, y: 4, z: 4, core: 2. Of those that a mesh axis runs over, the one named last changes fastest.
Arguments:
- grads: float32 [384, 65536], P(None, 'shard'), may hold values from -1200 to 1200
- owner: int32 [384, 1], replicated, may hold values from 0 to 127; in each aligned block of 384 rows (0 to 383, 384 to 767, ...) at most 8 rows name the same one
- left_stat: float32 [1024, 256, 256], P('shard'), may hold values from -60 to 640, as said below
- right_stat: float32 [1024, 256, 256], P('shard'), may hold values from -60 to 640, as said below
- left_root: bfloat16 [1024, 256, 256], P('shard'), may hold values from -1 to 2.5, as said below
- right_root: bfloat16 [1024, 256, 256], P('shard'), may hold values from -1 to 2.5, as said below
- moment: float32 [1024, 256, 256], P('shard'), may hold values from 0.1 to 10
Outputs:
- update: float32 [384, 65536], P(None, 'shard')
- left_new: float32 [1024, 256, 256], P('shard')
- right_new: float32 [1024, 256, 256], P('shard')
- moment_new: float32 [1024, 256, 256], P('shard')
Inputs may be any that keep to these rules, and one draw needn't show every extreme that they name: Every owner is named by at least one tile and by at most 8 tiles; some owner by exactly 8. `left_stat`: each matrix is symmetric. `right_stat`: each matrix is symmetric. `left_root`: each matrix is symmetric. `right_root`: each matrix is symmetric.
All inputs are finite; a program needn't handle non-finite values.
Results may differ from a plain program's by a relative error of at most 0.0041.
Values sent between devices are 32-bit elements; how exact they have to be, the bound alone decides.
No kernel may reach another device: no remote copies, remote signals or barrier semaphores. Data moves between devices by JAX's collectives and lax.ppermute only.
A program may use at most 64 MiB of HBM per device.

v0:
```python
import math

import jax
import jax.numpy as jnp
from jax import lax
from jax.sharding import PartitionSpec as P

B = 256
SLOT_DEV = 8


def positions(owner):
    owner_ids = owner[:, 0]
    tile_order = jnp.arange(owner_ids.shape[0], dtype=jnp.int32)
    earlier = (owner_ids[None, :] == owner_ids[:, None]) & (
        tile_order[None, :] < tile_order[:, None]
    )
    slot_rank = jnp.sum(earlier.astype(jnp.int32), axis=1)
    return owner_ids * SLOT_DEV + slot_rank


def shards(grads, owner, left_stat, right_stat, left_root, right_root, moment):
    devices = lax.axis_size("shard")
    slot_count = left_stat.shape[0]
    shard_len = grads.shape[1]
    target = positions(owner)
    clip_limit = math.sqrt(grads.shape[0] * shard_len * devices)
    squares_all = lax.psum(jnp.sum(grads * grads), "shard")
    clip_scale = clip_limit / jnp.sqrt(squares_all)
    outgoing = grads * clip_scale
    outbox = jnp.zeros((devices * slot_count, shard_len), jnp.float32).at[target].set(outgoing)
    outbox = outbox.reshape(devices, slot_count, shard_len)
    arrived = lax.all_to_all(outbox, "shard", split_axis=0, concat_axis=2, tiled=True)
    blocks = arrived.reshape(slot_count, B, B)
    highest = lax.Precision.HIGHEST
    left_new = 0.95 * left_stat + jnp.einsum(
        "sij,skj->sik", blocks, blocks, precision=highest, preferred_element_type=jnp.float32
    )
    right_new = 0.95 * right_stat + jnp.einsum(
        "sji,sjk->sik", blocks, blocks, precision=highest, preferred_element_type=jnp.float32
    )
    moment_new = 0.9 * moment + 0.1 * blocks * blocks
    adam_step = blocks / jnp.sqrt(moment_new)
    left_side = jnp.einsum(
        "sij,sjk->sik", left_root, blocks.astype(jnp.bfloat16), preferred_element_type=jnp.float32
    ).astype(jnp.bfloat16)
    shaped = jnp.einsum("sij,sjk->sik", left_side, right_root, preferred_element_type=jnp.float32)
    graft_ratio = jnp.sqrt(jnp.mean(adam_step * adam_step, axis=(1, 2))) / jnp.sqrt(
        jnp.mean(shaped * shaped, axis=(1, 2)) + 1e-06
    )
    scaled = (shaped * graft_ratio[:, None, None]).reshape(slot_count, devices, shard_len)
    returned = lax.all_to_all(scaled, "shard", split_axis=1, concat_axis=0, tiled=True)
    gathered_rows = returned.reshape(devices * slot_count, shard_len)
    update = gathered_rows[target]
    return (update, left_new, right_new, moment_new)


def solution(mesh):
    return jax.shard_map(
        shards,
        mesh=mesh,
        in_specs=(
            P(None, "shard"),
            P(),
            P("shard", None, None),
            P("shard", None, None),
            P("shard", None, None),
            P("shard", None, None),
            P("shard", None, None),
        ),
        out_specs=(
            P(None, "shard"),
            P("shard", None, None),
            P("shard", None, None),
            P("shard", None, None),
        ),
        check_vma=False,
    )
```

profile of v0, /device:TPU:1, one launch (start us, length us, event | category | flops | bytes accessed | tf_op | source)
XLA Modules:
  0.0 174.5 jit_solution(10387081859218523344)
XLA Ops:
  0.6 0.0 copy-start
  0.6 0.8 reduce
  1.4 0.2 convert_reduce_fusion
  1.7 1.9 %multiply_reduce_fusion.2 = f32[]{:T(128)} fusion(f32[384,512]{1,0:T(8,128)} %param.7), kind=kLoop, calls=%fused_computation.15 | loop fusion | flops 393215 | bytes 786436 | tf_op jit(solution)/shard_map/reduce_sum | solution.py:28
  3.6 0.7 fusion.9
  4.3 68.7 %psum.7 = f32[]{:T(128)} all-reduce(f32[]{:T(128)} %multiply_reduce_fusion.2), channel_id=1, replica_groups=mesh['shard'=128] {'shard'}, use_global_device_ids=true, to_apply=%region_2.0 | all-reduce | flops 1 | bytes 8 | tf_op jit(solution)/shard_map/psum | solution.py:28
  73.7 3.0 %scatter_custom_fusion = f32[1024,512]{1,0:T(8,128)S(1)} fusion(s32[384]{0:T(512)S(1)} %fusion.9, f32[]{:T(128)} %constant.10.clone.1, f32[384,512]{1,0:T(8,128)} %param.7, f32[]{:T(128)S(6)} %div.15), kind=kCustom, calls=%fused_computation.12 | custom fusion | flops 196608 | bytes 2883592 | tf_op jit(solution)/shard_map/scatter | solution.py:31
  76.7 34.9 %all_to_all.30 = f32[128,8,512]{2,1,0:T(8,128)S(1)} all-to-all(f32[128,8,512]{2,1,0:T(8,128)S(1)} %bitcast.18), channel_id=1, replica_groups=mesh['shard'=128] {'shard'}, dimensions={0} | all-to-all | bytes 4194304 | tf_op jit(solution)/shard_map/all_to_all | solution.py:33
  111.6 2.5 %copy.28 = f32[1,8,128,512]{3,2,1,0:T(8,128)} copy(f32[1,8,128,512]{3,1,2,0:T(8,128)S(1)} %bitcast.19) | data formatting | bytes 4194304 | tf_op jit(solution)/shard_map/all_to_all | solution.py:33
  114.2 1.7 reshape.35
  115.9 1.4 copy.29
  117.3 3.5 %multiply_reduce_fusion.1 = (f32[8]{0:T(128)S(1)}, f32[8,256,256]{2,1,0:T(8,128)}) fusion(f32[8,256,256]{2,1,0:T(8,128)S(1)} %reshape.35, f32[8,256,256]{2,1,0:T(8,128)} %param.13), kind=kLoop, calls=%fused_computation.7 | loop fusion | flops 3670008 | bytes 6291488 | tf_op jit(solution)/shard_map/reduce_sum | solution.py:48
  120.7 0.0 copy-done
  120.7 3.6 %multiply_reduce_fusion = (f32[8]{0:T(128)S(1)}, f32[8,256,256]{2,1,0:T(8,128)}) fusion(bf16[8,256,256]{2,1,0:T(8,128)(2,1)S(1)} %copy-done, bf16[8,256,256]{2,1,0:T(8,128)(2,1)} %param.11, bf16[8,256,256]{1,2,0:T(8,128)(2,1)} %copy.29), kind=kOutput, calls=%fused_computation.6 | convolution fusion | flops 538443776 | bytes 5242912 | tf_op jit(solution)/shard_map/sij,sjk->sik/dot_general | solution.py:47
  124.4 3.2 %broadcast_multiply_fusion = f32[8,256,256]{2,1,0:T(8,128)} fusion(f32[8,256,256]{2,1,0:T(8,128)} %get-tuple-element.11, f32[8]{0:T(128)S(1)} %rsqrt_multiply_fusion), kind=kLoop, calls=%fused_computation.10 | loop fusion | flops 524288 | bytes 4194336 | tf_op jit(solution)/shard_map/mul | solution.py:51
  127.6 2.9 %reshape.36 = f32[8,128,512]{2,1,0:T(8,128)} reshape(f32[8,256,256]{2,1,0:T(8,128)} %broadcast_multiply_fusion) | data formatting | bytes 4194304 | tf_op jit(solution)/shard_map/reshape | solution.py:51
  130.4 4.1 %copy.31 = f32[8,128,512]{2,0,1:T(8,128)} copy(f32[8,128,512]{2,1,0:T(8,128)} %reshape.36) | data formatting | bytes 4194304 | tf_op jit(solution)/shard_map/reshape | solution.py:51
  134.5 5.6 %all-to-all-start.1 = ((f32[8,128,512]{2,0,1:T(8,128)}), f32[8,128,512]{2,0,1:T(8,128)}, u32[]{:S(2)}, u32[]{:S(2)}) async-start(f32[8,128,512]{2,0,1:T(8,128)} %copy.31), calls=%async_computation.1 | async-start | bytes 4194304 | tf_op jit(solution)/shard_map/all_to_all | solution.py:52
  140.2 0.0 copy-start.1
  140.2 6.6 %multiply_add_fusion = f32[8,256,256]{2,1,0:T(8,128)} fusion(f32[8,256,256]{2,1,0:T(8,128)} %param.10, f32[8,256,256]{2,1,0:T(8,128)S(1)} %reshape.35), kind=kOutput, calls=%fused_computation.4 | convolution fusion | flops 1611661312 | bytes 6291456 | tf_op jit(solution)/shard_map/sji,sjk->sik/dot_general | solution.py:39
  146.7 0.0 copy-done.1
  146.7 3.6 %multiply_add_fusion.1 = f32[8,256,256]{2,1,0:T(8,128)} fusion(f32[8,256,256]{2,1,0:T(8,128)S(1)} %copy-done.1, f32[8,256,256]{2,1,0:T(8,128)S(1)} %reshape.35), kind=kOutput, calls=%fused_computation.5 | convolution fusion | flops 1611661312 | bytes 6291456 | tf_op jit(solution)/shard_map/sij,skj->sik/dot_general | solution.py:36
  150.4 19.9 %all-to-all-done.1 = f32[8,128,512]{2,0,1:T(8,128)} async-done(((f32[8,128,512]{2,0,1:T(8,128)}), f32[8,128,512]{2,0,1:T(8,128)}, u32[]{:S(2)}, u32[]{:S(2)}) %all-to-all-start.1) | async-done | bytes 2097184 | tf_op jit(solution)/shard_map/all_to_all | solution.py:52
  170.3 4.2 %gather_fusion = f32[384,512]{1,0:T(8,128)} fusion(f32[1024,512]{1,0:T(8,128)} %bitcast.5, s32[1024]{0:T(1024)S(1)} %pad_clamp_fusion), kind=kCustom, calls=%fused_computation | custom fusion | bytes 1574400 | tf_op jit(solution)/shard_map/gather | solution.py:54
  (2 shorter events, 0.0 us)
Async XLA Ops:
  0.6 120.1 %copy-start = (bf16[8,256,256]{2,1,0:T(8,128)(2,1)S(1)}, bf16[8,256,256]{2,1,0:T(8,128)(2,1)}, u32[]{:S(2)}) copy-start(bf16[8,256,256]{2,1,0:T(8,128)(2,1)} %param.12) | copy-start | bytes 3145732
  134.5 35.8 %all-to-all-start.1 = ((f32[8,128,512]{2,0,1:T(8,128)}), f32[8,128,512]{2,0,1:T(8,128)}, u32[]{:S(2)}, u32[]{:S(2)}) async-start(f32[8,128,512]{2,0,1:T(8,128)} %copy.31), calls=%async_computation.1 | async-start | bytes 4194304 | tf_op jit(solution)/shard_map/all_to_all | solution.py:52
  140.2 6.6 %copy-start.1 = (f32[8,256,256]{2,1,0:T(8,128)S(1)}, f32[8,256,256]{2,1,0:T(8,128)}, u32[]{:S(2)}) copy-start(f32[8,256,256]{2,1,0:T(8,128)} %param.9) | copy-start | bytes 6291460
where the time goes:
time: 175 us
  blocking collectives  104 us (59%)
  waiting for transfers between devices  19.9 us (11%)
  local copies, waits for them, and re-layouts  16.8 us (10%)
  matrix products  13.8 us (8%)
  other arithmetic  13.3 us (8%)
  starting transfers between devices  5.62 us (3%)
    psum x1, blocking collectives, shards(): squares_all = lax.psum(jnp.sum(grads * grads), 'shard')  68.7 us
    all_to_all x1, blocking collectives, shards(): lax.all_to_all(outbox, 'shard', split_axis=0, concat_axis=2, tiled=True)  34.9 us
    all_to_all x1, waiting for transfers between devices, shards(): lax.all_to_all(scaled, 'shard', split_axis=1, concat_axis=0, tiled=True)  19.9 us
    reshape x2, local copies, waits for them, and re-layouts, shards(): (shaped * graft_ratio[:, None, None]).reshape(slot_count, devices, shard_...  6.96 us
    dot_general x1, matrix products, shards(): jnp.einsum('sji,sjk->sik', blocks, blocks, precision=highest, preferred_e...  6.56 us
    all_to_all x1, starting transfers between devices, shards(): lax.all_to_all(scaled, 'shard', split_axis=1, concat_axis=0, tiled=True)  5.62 us
    gather x1, local copies, waits for them, and re-layouts, shards(): update = gathered_rows[target]  4.23 us
    dot_general x1, matrix products, shards(): jnp.einsum('sij,skj->sik', blocks, blocks, precision=highest, preferred_e...  3.64 us
  transfers between devices with their start and end apart: 1, of which 1 were waited for; matrix products, arithmetic and copies ran while one was open for 6% of the time, Pallas kernels for 0%

commit v1 on v0

--- a/solution.py
+++ b/solution.py
@@ -19,19 +19,36 @@
     return owner_ids * SLOT_DEV + slot_rank
 
 
+def total_over(value, axis_name, sizes):
+    devices = lax.axis_size(axis_name)
+    step = 1
+    for size in sizes:
+        block = step * size
+        parts = [value]
+        for shift in range(1, size):
+            pairs = [
+                (d, d // block * block + (d % block + shift * step) % block)
+                for d in range(devices)
+            ]
+            parts.append(lax.ppermute(value, axis_name, pairs))
+        value = sum(parts[1:], parts[0])
+        step = block
+    return value
+
+
 def shards(grads, owner, left_stat, right_stat, left_root, right_root, moment):
     devices = lax.axis_size("shard")
     slot_count = left_stat.shape[0]
     shard_len = grads.shape[1]
     target = positions(owner)
     clip_limit = math.sqrt(grads.shape[0] * shard_len * devices)
-    squares_all = lax.psum(jnp.sum(grads * grads), "shard")
-    clip_scale = clip_limit / jnp.sqrt(squares_all)
-    outgoing = grads * clip_scale
-    outbox = jnp.zeros((devices * slot_count, shard_len), jnp.float32).at[target].set(outgoing)
+    squares = jnp.sum(jnp.square(grads).reshape(-1, 8, 128), axis=0)
+    outbox = jnp.zeros((devices * slot_count, shard_len), jnp.float32).at[target].set(grads)
     outbox = outbox.reshape(devices, slot_count, shard_len)
     arrived = lax.all_to_all(outbox, "shard", split_axis=0, concat_axis=2, tiled=True)
-    blocks = arrived.reshape(slot_count, B, B)
+    squares_all = jnp.sum(total_over(squares, "shard", (2, 4, 4, 4)))
+    clip_scale = clip_limit / jnp.sqrt(squares_all)
+    blocks = arrived.reshape(slot_count, B, B) * clip_scale
     highest = lax.Precision.HIGHEST
     left_new = 0.95 * left_stat + jnp.einsum(
         "sij,skj->sik", blocks, blocks, precision=highest, preferred_element_type=jnp.float32

time: 175 us -> 126 us (0.72)
  blocking collectives: 104 us -> 0 us
  starting transfers between devices: 5.62 us -> 39.4 us
  waiting for transfers between devices: 19.9 us -> 35.3 us
  local copies, waits for them, and re-layouts: 16.8 us -> 22.7 us
    psum x1 -> x0, blocking collectives: 68.7 us -> none  [shards(): squares_all = lax.psum(jnp.sum(grads * grads), 'shard')]
    all_to_all x1 -> x0, blocking collectives: 34.9 us -> none  [shards(): lax.all_to_all(outbox, 'shard', split_axis=0, concat_axis=2, tiled=True)]
    ppermute x0 -> x10, starting transfers between devices: none -> 16.7 us  [total_over(): parts.append(lax.ppermute(value, axis_name, pairs))]
    ppermute x0 -> x10, waiting for transfers between devices: none -> 15.5 us  [total_over(): parts.append(lax.ppermute(value, axis_name, pairs))]
    all_to_all x0 -> x1, starting transfers between devices: none -> 11.5 us  [shards(): lax.all_to_all(outbox, 'shard', split_axis=0, concat_axis=2, tiled=True)]
    mul x0 -> x3, local copies, waits for them, and re-layouts: none -> 5.65 us  [shards(): blocks = arrived.reshape(slot_count, B, B) * clip_scale]
    all_to_all x1, starting transfers between devices: 5.62 us -> 11.2 us  [shards(): lax.all_to_all(scaled, 'shard', split_axis=1, concat_axis=0, tiled=True)]
    scatter x0 -> x1, local copies, waits for them, and re-layouts: none -> 3.82 us  [shards(): jnp.zeros((devices * slot_count, shard_len), jnp.float32).at[target]]
  transfers between devices with their start and end apart: 1 -> 12, of which waited for: 1 -> 9; matrix products, arithmetic and copies ran while one was open for 6% -> 13% of each run, Pallas kernels for 0% -> 0%
where the time goes in v1:
time: 126 us
  starting transfers between devices  39.4 us (31%)
  waiting for transfers between devices  35.3 us (28%)
  local copies, waits for them, and re-layouts  22.7 us (18%)
  matrix products  13.8 us (11%)
  other arithmetic  13 us (10%)
  between operations  1.41 us (1%)
    all_to_all x1, waiting for transfers between devices, shards(): lax.all_to_all(scaled, 'shard', split_axis=1, concat_axis=0, tiled=True)  19.8 us
    ppermute x10, starting transfers between devices, total_over(): parts.append(lax.ppermute(value, axis_name, pairs))  16.7 us
    ppermute x10, waiting for transfers between devices, total_over(): parts.append(lax.ppermute(value, axis_name, pairs))  15.5 us
    all_to_all x1, starting transfers between devices, shards(): lax.all_to_all(outbox, 'shard', split_axis=0, concat_axis=2, tiled=True)  11.5 us
    all_to_all x1, starting transfers between devices, shards(): lax.all_to_all(scaled, 'shard', split_axis=1, concat_axis=0, tiled=True)  11.2 us
    reshape x2, local copies, waits for them, and re-layouts, shards(): (shaped * graft_ratio[:, None, None]).reshape(slot_count, devices, shard_...  6.96 us
    dot_general x1, matrix products, shards(): jnp.einsum('sji,sjk->sik', blocks, blocks, precision=highest, preferred_e...  6.56 us
    mul x3, local copies, waits for them, and re-layouts, shards(): blocks = arrived.reshape(slot_count, B, B) * clip_scale  5.65 us
  transfers between devices with their start and end apart: 12, of which 9 were waited for; matrix products, arithmetic and copies ran while one was open for 13% of the time, Pallas kernels for 0%

profile of v1, /device:TPU:1, one launch (start us, length us, event | category | flops | bytes accessed | tf_op | source)
XLA Modules:
  0.0 125.8 jit_solution(13064296477991715307)
XLA Ops:
  0.6 0.0 copy-start
  0.6 0.8 reduce
  1.4 0.2 convert_reduce_fusion
  1.7 0.7 fusion.7
  2.4 3.8 %scatter_custom_fusion = f32[1024,512]{1,0:T(8,128)} fusion(s32[384]{0:T(512)S(1)} %fusion.7, f32[384,512]{1,0:T(8,128)} %param.7, f32[]{:T(128)} %constant.10.clone.1), kind=kCustom, calls=%fused_computation.13 | custom fusion | bytes 2097664 | tf_op jit(solution)/shard_map/scatter | solution.py:46
  6.2 11.5 %all-to-all-start = ((f32[128,8,512]{2,1,0:T(8,128)}), f32[128,8,512]{2,1,0:T(8,128)S(1)}, u32[]{:S(2)}, u32[]{:S(2)}) async-start(f32[128,8,512]{2,1,0:T(8,128)} %bitcast.19), calls=%async_computation | async-start | bytes 4194304 | tf_op jit(solution)/shard_map/all_to_all | solution.py:48
  17.7 2.4 %square.3 = f32[384,512]{1,0:T(8,128)} multiply(f32[384,512]{1,0:T(8,128)} %param.7, f32[384,512]{1,0:T(8,128)} %param.7) | non-fusion elementwise | flops 196608 | bytes 2359296 | tf_op jit(solution)/shard_map/square | solution.py:45
  20.1 2.1 %reshape.40 = f32[192,8,128]{2,1,0:T(8,128)} reshape(f32[384,512]{1,0:T(8,128)} %square.3) | data formatting | bytes 1572864 | tf_op jit(solution)/shard_map/reshape | solution.py:45
  22.2 1.3 %reduce_sum.49 = f32[8,128]{1,0:T(8,128)S(1)} reduce(f32[192,8,128]{2,1,0:T(8,128)} %reshape.40, f32[]{:T(128)} %constant.10.clone.1), dimensions={0}, to_apply=%region_2.0 | reduce | flops 195584 | bytes 790532 | tf_op jit(solution)/shard_map/reduce_sum | solution.py:45
  23.5 1.1 collective-permute-start
  24.7 0.8 collective-permute-done
  25.5 0.7 collective-permute-start.1
  26.2 2.4 %collective-permute-start.2 = (f32[8,128]{1,0:T(8,128)S(1)}, f32[8,128]{1,0:T(8,128)S(1)}, u32[]{:S(2)}, u32[]{:S(2)}) collective-permute-start(f32[8,128]{1,0:T(8,128)S(1)} %add.57), channel_id=1, source_target_pairs={{0,4},{1,5},{2,6},{3,7},{4,0},{5,1},{6,2},{7,3},{8,12},{9,13},{10,... | collective-permute-start | bytes 12296 | tf_op jit(solution)/shard_map/ppermute | solution.py:33
  28.6 1.1 collective-permute-start.3
  29.8 0.9 collective-permute-done.1
  30.6 6.5 %collective-permute-done.2 = f32[8,128]{1,0:T(8,128)S(1)} collective-permute-done((f32[8,128]{1,0:T(8,128)S(1)}, f32[8,128]{1,0:T(8,128)S(1)}, u32[]{:S(2)}, u32[]{:S(2)}) %collective-permute-start.2) | collective-permute-done | bytes 4128 | tf_op jit(solution)/shard_map/ppermute | solution.py:33
  37.2 0.3 collective-permute-done.3
  37.5 0.5 collective-permute-start.4
  38.0 3.8 %collective-permute-start.5 = (f32[8,128]{1,0:T(8,128)S(1)}, f32[8,128]{1,0:T(8,128)S(1)}, u32[]{:S(2)}, u32[]{:S(2)}) collective-permute-start(f32[8,128]{1,0:T(8,128)S(1)} %add_add_fusion.1), channel_id=1, source_target_pairs={{0,16},{1,17},{2,18},{3,19},{4,20},{5,21},{6,22},{7,23},{8,24},{9,... | collective-permute-start | bytes 12296 | tf_op jit(solution)/shard_map/ppermute | solution.py:33
  41.8 0.0 collective-permute-start.6
  41.8 0.3 collective-permute-done.4
  42.1 4.4 %collective-permute-done.5 = f32[8,128]{1,0:T(8,128)S(1)} collective-permute-done((f32[8,128]{1,0:T(8,128)S(1)}, f32[8,128]{1,0:T(8,128)S(1)}, u32[]{:S(2)}, u32[]{:S(2)}) %collective-permute-start.5) | collective-permute-done | bytes 4128 | tf_op jit(solution)/shard_map/ppermute | solution.py:33
  46.5 0.0 collective-permute-done.6
  46.5 2.2 %collective-permute-start.7 = (f32[8,128]{1,0:T(8,128)S(1)}, f32[8,128]{1,0:T(8,128)S(1)}, u32[]{:S(2)}, u32[]{:S(2)}) collective-permute-start(f32[8,128]{1,0:T(8,128)S(1)} %add_add_fusion), channel_id=1, source_target_pairs={{0,32},{1,33},{2,34},{3,35},{4,36},{5,37},{6,38},{7,39},{8,40},{9,... | collective-permute-start | bytes 12296 | tf_op jit(solution)/shard_map/ppermute | solution.py:33
  48.7 4.7 %collective-permute-start.8 = (f32[8,128]{1,0:T(8,128)S(1)}, f32[8,128]{1,0:T(8,128)S(1)}, u32[]{:S(2)}, u32[]{:S(2)}) collective-permute-start(f32[8,128]{1,0:T(8,128)S(1)} %add_add_fusion), channel_id=1, source_target_pairs={{0,64},{1,65},{2,66},{3,67},{4,68},{5,69},{6,70},{7,71},{8,72},{9,... | collective-permute-start | bytes 12296 | tf_op jit(solution)/shard_map/ppermute | solution.py:33
  53.4 0.2 collective-permute-start.9
  53.5 0.0 collective-permute-done.7
  53.6 0.9 collective-permute-done.8
  54.4 1.4 %collective-permute-done.9 = f32[8,128]{1,0:T(8,128)S(1)} collective-permute-done((f32[8,128]{1,0:T(8,128)S(1)}, f32[8,128]{1,0:T(8,128)S(1)}, u32[]{:S(2)}, u32[]{:S(2)}) %collective-permute-start.9) | collective-permute-done | bytes 4128 | tf_op jit(solution)/shard_map/ppermute | solution.py:33
  55.8 0.6 add_reduce_fusion
  57.1 0.0 all-to-all-done
  57.1 0.2 multiply_bitcast_fusion
  57.4 2.5 %copy.28 = f32[1,8,128,512]{3,2,1,0:T(8,128)} copy(f32[1,8,128,512]{3,1,2,0:T(8,128)S(1)} %multiply_bitcast_fusion) | data formatting | bytes 4194304 | tf_op jit(solution)/shard_map/mul | solution.py:51
  59.9 1.7 %mul.63 = f32[8,256,256]{2,1,0:T(8,128)S(1)} reshape(f32[1,8,128,512]{3,2,1,0:T(8,128)} %copy.28) | data formatting | bytes 4194304 | tf_op jit(solution)/shard_map/mul | solution.py:51
  61.7 1.4 %copy.29 = bf16[8,256,256]{1,2,0:T(8,128)(2,1)} copy(f32[8,256,256]{2,1,0:T(8,128)S(1)} %mul.63) | data formatting | bytes 3145728 | tf_op jit(solution)/shard_map/mul | solution.py:51
  63.0 3.5 %multiply_reduce_fusion.1 = (f32[8]{0:T(128)S(1)}, f32[8,256,256]{2,1,0:T(8,128)}) fusion(f32[8,256,256]{2,1,0:T(8,128)S(1)} %mul.63, f32[8,256,256]{2,1,0:T(8,128)} %param.13), kind=kLoop, calls=%fused_computation.7 | loop fusion | flops 3670008 | bytes 6291488 | tf_op jit(solution)/shard_map/reduce_sum | solution.py:65
  66.5 0.0 copy-done
  66.5 3.6 %multiply_reduce_fusion = (f32[8]{0:T(128)S(1)}, f32[8,256,256]{2,1,0:T(8,128)}) fusion(bf16[8,256,256]{2,1,0:T(8,128)(2,1)S(1)} %copy-done, bf16[8,256,256]{2,1,0:T(8,128)(2,1)} %param.11, bf16[8,256,256]{1,2,0:T(8,128)(2,1)} %copy.29), kind=kOutput, calls=%fused_computation.6 | convolution fusion | flops 538443776 | bytes 5242912 | tf_op jit(solution)/shard_map/sij,sjk->sik/dot_general | solution.py:64
  70.1 3.2 %broadcast_multiply_fusion = f32[8,256,256]{2,1,0:T(8,128)} fusion(f32[8,256,256]{2,1,0:T(8,128)} %get-tuple-element.11, f32[8]{0:T(128)S(1)} %rsqrt_multiply_fusion), kind=kLoop, calls=%fused_computation.11 | loop fusion | flops 524288 | bytes 4194336 | tf_op jit(solution)/shard_map/mul | solution.py:68
  73.3 2.9 %reshape.41 = f32[8,128,512]{2,1,0:T(8,128)} reshape(f32[8,256,256]{2,1,0:T(8,128)} %broadcast_multiply_fusion) | data formatting | bytes 4194304 | tf_op jit(solution)/shard_map/reshape | solution.py:68
  76.2 4.1 %copy.31 = f32[8,128,512]{2,0,1:T(8,128)} copy(f32[8,128,512]{2,1,0:T(8,128)} %reshape.41) | data formatting | bytes 4194304 | tf_op jit(solution)/shard_map/reshape | solution.py:68
  80.3 11.2 %all-to-all-start.1 = ((f32[8,128,512]{2,0,1:T(8,128)}), f32[8,128,512]{2,0,1:T(8,128)}, u32[]{:S(2)}, u32[]{:S(2)}) async-start(f32[8,128,512]{2,0,1:T(8,128)} %copy.31), calls=%async_computation.1 | async-start | bytes 4194304 | tf_op jit(solution)/shard_map/all_to_all | solution.py:69
  91.5 0.0 copy-start.1
  91.5 6.6 %multiply_add_fusion = f32[8,256,256]{2,1,0:T(8,128)} fusion(f32[8,256,256]{2,1,0:T(8,128)} %param.10, f32[8,256,256]{2,1,0:T(8,128)S(1)} %mul.63), kind=kOutput, calls=%fused_computation.4 | convolution fusion | flops 1611661312 | bytes 6291456 | tf_op jit(solution)/shard_map/sji,sjk->sik/dot_general | solution.py:56
  98.1 0.0 copy-done.1
  98.1 3.6 %multiply_add_fusion.1 = f32[8,256,256]{2,1,0:T(8,128)} fusion(f32[8,256,256]{2,1,0:T(8,128)S(1)} %copy-done.1, f32[8,256,256]{2,1,0:T(8,128)S(1)} %mul.63), kind=kOutput, calls=%fused_computation.5 | convolution fusion | flops 1611661312 | bytes 6291456 | tf_op jit(solution)/shard_map/sij,skj->sik/dot_general | solution.py:53
  101.7 19.8 %all-to-all-done.1 = f32[8,128,512]{2,0,1:T(8,128)} async-done(((f32[8,128,512]{2,0,1:T(8,128)}), f32[8,128,512]{2,0,1:T(8,128)}, u32[]{:S(2)}, u32[]{:S(2)}) %all-to-all-start.1) | async-done | bytes 2097184 | tf_op jit(solution)/shard_map/all_to_all | solution.py:69
  121.5 4.2 %gather_fusion = f32[384,512]{1,0:T(8,128)} fusion(f32[1024,512]{1,0:T(8,128)} %bitcast.5, s32[1024]{0:T(1024)S(1)} %pad_clamp_fusion), kind=kCustom, calls=%fused_computation | custom fusion | bytes 1574400 | tf_op jit(solution)/shard_map/gather | solution.py:71
  (5 shorter events, 0.0 us)
Async XLA Ops:
  0.6 65.9 %copy-start = (bf16[8,256,256]{2,1,0:T(8,128)(2,1)S(1)}, bf16[8,256,256]{2,1,0:T(8,128)(2,1)}, u32[]{:S(2)}) copy-start(bf16[8,256,256]{2,1,0:T(8,128)(2,1)} %param.12) | copy-start | bytes 3145732
  6.2 50.9 %all-to-all-start = ((f32[128,8,512]{2,1,0:T(8,128)}), f32[128,8,512]{2,1,0:T(8,128)S(1)}, u32[]{:S(2)}, u32[]{:S(2)}) async-start(f32[128,8,512]{2,1,0:T(8,128)} %bitcast.19), calls=%async_computation | async-start | bytes 4194304 | tf_op jit(solution)/shard_map/all_to_all | solution.py:48
  23.5 2.0 %collective-permute-start = (f32[8,128]{1,0:T(8,128)S(1)}, f32[8,128]{1,0:T(8,128)S(1)}, u32[]{:S(2)}, u32[]{:S(2)}) collective-permute-start(f32[8,128]{1,0:T(8,128)S(1)} %reduce_sum.49), channel_id=1, source_target_pairs={{0,1},{1,0},{2,3},{3,2},{4,5},{5,4},{6,7},{7,6},{8,9},{9,8},{10,11... | collective-permute-start | bytes 12296 | tf_op jit(solution)/shard_map/ppermute | solution.py:33
  25.5 5.1 %collective-permute-start.1 = (f32[8,128]{1,0:T(8,128)S(1)}, f32[8,128]{1,0:T(8,128)S(1)}, u32[]{:S(2)}, u32[]{:S(2)}) collective-permute-start(f32[8,128]{1,0:T(8,128)S(1)} %add.57), channel_id=1, source_target_pairs={{0,2},{1,3},{2,4},{3,5},{4,6},{5,7},{6,0},{7,1},{8,10},{9,11},{10,... | collective-permute-start | bytes 12296 | tf_op jit(solution)/shard_map/ppermute | solution.py:33
  26.2 11.0 %collective-permute-start.2 = (f32[8,128]{1,0:T(8,128)S(1)}, f32[8,128]{1,0:T(8,128)S(1)}, u32[]{:S(2)}, u32[]{:S(2)}) collective-permute-start(f32[8,128]{1,0:T(8,128)S(1)} %add.57), channel_id=1, source_target_pairs={{0,4},{1,5},{2,6},{3,7},{4,0},{5,1},{6,2},{7,3},{8,12},{9,13},{10,... | collective-permute-start | bytes 12296 | tf_op jit(solution)/shard_map/ppermute | solution.py:33
  28.6 8.9 %collective-permute-start.3 = (f32[8,128]{1,0:T(8,128)S(1)}, f32[8,128]{1,0:T(8,128)S(1)}, u32[]{:S(2)}, u32[]{:S(2)}) collective-permute-start(f32[8,128]{1,0:T(8,128)S(1)} %add.57), channel_id=1, source_target_pairs={{0,6},{1,7},{2,0},{3,1},{4,2},{5,3},{6,4},{7,5},{8,14},{9,15},{10,... | collective-permute-start | bytes 12296 | tf_op jit(solution)/shard_map/ppermute | solution.py:33
  37.5 4.6 %collective-permute-start.4 = (f32[8,128]{1,0:T(8,128)S(1)}, f32[8,128]{1,0:T(8,128)S(1)}, u32[]{:S(2)}, u32[]{:S(2)}) collective-permute-start(f32[8,128]{1,0:T(8,128)S(1)} %add_add_fusion.1), channel_id=1, source_target_pairs={{0,8},{1,9},{2,10},{3,11},{4,12},{5,13},{6,14},{7,15},{8,16},{9,17... | collective-permute-start | bytes 12296 | tf_op jit(solution)/shard_map/ppermute | solution.py:33
  38.0 8.5 %collective-permute-start.5 = (f32[8,128]{1,0:T(8,128)S(1)}, f32[8,128]{1,0:T(8,128)S(1)}, u32[]{:S(2)}, u32[]{:S(2)}) collective-permute-start(f32[8,128]{1,0:T(8,128)S(1)} %add_add_fusion.1), channel_id=1, source_target_pairs={{0,16},{1,17},{2,18},{3,19},{4,20},{5,21},{6,22},{7,23},{8,24},{9,... | collective-permute-start | bytes 12296 | tf_op jit(solution)/shard_map/ppermute | solution.py:33
  41.8 4.7 %collective-permute-start.6 = (f32[8,128]{1,0:T(8,128)S(1)}, f32[8,128]{1,0:T(8,128)S(1)}, u32[]{:S(2)}, u32[]{:S(2)}) collective-permute-start(f32[8,128]{1,0:T(8,128)S(1)} %add_add_fusion.1), channel_id=1, source_target_pairs={{0,24},{1,25},{2,26},{3,27},{4,28},{5,29},{6,30},{7,31},{8,0},{9,1... | collective-permute-start | bytes 12296 | tf_op jit(solution)/shard_map/ppermute | solution.py:33
  46.5 7.1 %collective-permute-start.7 = (f32[8,128]{1,0:T(8,128)S(1)}, f32[8,128]{1,0:T(8,128)S(1)}, u32[]{:S(2)}, u32[]{:S(2)}) collective-permute-start(f32[8,128]{1,0:T(8,128)S(1)} %add_add_fusion), channel_id=1, source_target_pairs={{0,32},{1,33},{2,34},{3,35},{4,36},{5,37},{6,38},{7,39},{8,40},{9,... | collective-permute-start | bytes 12296 | tf_op jit(solution)/shard_map/ppermute | solution.py:33
  48.7 5.7 %collective-permute-start.8 = (f32[8,128]{1,0:T(8,128)S(1)}, f32[8,128]{1,0:T(8,128)S(1)}, u32[]{:S(2)}, u32[]{:S(2)}) collective-permute-start(f32[8,128]{1,0:T(8,128)S(1)} %add_add_fusion), channel_id=1, source_target_pairs={{0,64},{1,65},{2,66},{3,67},{4,68},{5,69},{6,70},{7,71},{8,72},{9,... | collective-permute-start | bytes 12296 | tf_op jit(solution)/shard_map/ppermute | solution.py:33
  53.4 2.5 %collective-permute-start.9 = (f32[8,128]{1,0:T(8,128)S(1)}, f32[8,128]{1,0:T(8,128)S(1)}, u32[]{:S(2)}, u32[]{:S(2)}) collective-permute-start(f32[8,128]{1,0:T(8,128)S(1)} %add_add_fusion), channel_id=1, source_target_pairs={{0,96},{1,97},{2,98},{3,99},{4,100},{5,101},{6,102},{7,103},{8,104... | collective-permute-start | bytes 12296 | tf_op jit(solution)/shard_map/ppermute | solution.py:33
  80.3 41.3 %all-to-all-start.1 = ((f32[8,128,512]{2,0,1:T(8,128)}), f32[8,128,512]{2,0,1:T(8,128)}, u32[]{:S(2)}, u32[]{:S(2)}) async-start(f32[8,128,512]{2,0,1:T(8,128)} %copy.31), calls=%async_computation.1 | async-start | bytes 4194304 | tf_op jit(solution)/shard_map/all_to_all | solution.py:69
  91.5 6.6 %copy-start.1 = (f32[8,256,256]{2,1,0:T(8,128)S(1)}, f32[8,256,256]{2,1,0:T(8,128)}, u32[]{:S(2)}) copy-start(f32[8,256,256]{2,1,0:T(8,128)} %param.9) | copy-start | bytes 6291460

commit v2 on v0

v2 whole, which is shorter than its diff:
```python
import functools
import math

import jax
import jax.numpy as jnp
from jax import lax
from jax.experimental import pallas as pl
from jax.experimental.pallas import tpu as pltpu
from jax.sharding import PartitionSpec as P

B = 256
SLOT_DEV = 8
LANES = 128
OUT_ROW = 2 * SLOT_DEV + 1
BACK_ROW = 2 * SLOT_DEV

ANY = pl.BlockSpec(memory_space=pl.ANY)
VMEM = pl.BlockSpec(memory_space=pltpu.VMEM)
SMEM = pl.BlockSpec(memory_space=pltpu.SMEM)
F32 = jnp.float32
BF16 = jnp.bfloat16


def call(kernel, in_specs, out_specs, out_shape, scratch, flops, bytes_accessed, vmem_mib=56):
    return pl.pallas_call(
        kernel,
        in_specs=in_specs,
        out_specs=out_specs,
        out_shape=out_shape,
        scratch_shapes=scratch,
        cost_estimate=pl.CostEstimate(flops=flops, bytes_accessed=bytes_accessed, transcendentals=0),
        compiler_params=pltpu.CompilerParams(vmem_limit_bytes=vmem_mib * 1024 * 1024),
    )


def started(source, target, sem):
    copy = pltpu.make_async_copy(source, target, sem)
    copy.start()
    return copy


def three_terms(x):
    high = x.astype(BF16)
    rest = x - high.astype(F32)
    middle = rest.astype(BF16)
    low = (rest - middle.astype(F32)).astype(BF16)
    return high, middle, low


def dot(a, b):
    return jnp.dot(a, b, preferred_element_type=F32)


def fold(x):
    total = jnp.sum(x.reshape(-1, 8, x.shape[1]), axis=0)
    return sum(total[:, lane : lane + LANES] for lane in range(0, x.shape[1], LANES))


def total_of(x):
    return jnp.sum(jnp.sum(x, axis=0, keepdims=True), axis=1, keepdims=True)


def pack_kernel(chunks, owner_hbm, grads_hbm, box, place_ref, owner, grads, sems):
    copies = [started(owner_hbm, owner, sems.at[0]), started(grads_hbm, grads, sems.at[1])]
    tiles = grads.shape[0]
    message = 2 * OUT_ROW
    copies[0].wait()
    owner_row = owner[...].astype(F32)
    owner_col = jnp.transpose(jnp.broadcast_to(owner_row, (8, tiles)))[:, :1]
    sub = lax.broadcasted_iota(jnp.int32, (tiles, tiles), 0)
    lane = lax.broadcasted_iota(jnp.int32, (tiles, tiles), 1)
    earlier = (owner_col == owner_row) & (sub < lane)
    rank = jnp.sum(earlier.astype(F32), axis=0, keepdims=True)
    place = rank * LANES + owner_row
    back = rank * 2 + owner_row * (2 * BACK_ROW)
    place_ref[...] = jnp.broadcast_to(back, (8, tiles)).astype(jnp.int32)
    copies[1].wait()
    squares = jnp.sum(fold(jnp.square(grads[...])), axis=0, keepdims=True)
    box[pl.ds(OUT_ROW - 1, LANES, stride=message), :] = jnp.broadcast_to(squares, (LANES, LANES))
    box[pl.ds(message - 1, LANES, stride=message), :] = jnp.zeros((LANES, LANES), F32)
    terms = jnp.concatenate(three_terms(grads[...]), axis=0)
    dests = LANES // chunks
    sub = lax.broadcasted_iota(jnp.int32, (SLOT_DEV * dests, tiles), 0)
    slots = (sub // dests * LANES + sub % dests).astype(F32)
    for k in range(chunks):
        chosen = (slots == place - float(k * dests)).astype(BF16)
        sent = dot(jnp.concatenate([chosen] * 3, axis=1), terms)
        for s in range(SLOT_DEV):
            for q in range(4):
                at = k * dests * message + q // 2 * OUT_ROW + 2 * s + q % 2
                box[pl.ds(at, dests, stride=message), :] = sent[
                    s * dests : (s + 1) * dests, q * LANES : (q + 1) * LANES
                ]


def clip_of(limit, box):
    squares = box[pl.ds(OUT_ROW - 1, LANES, stride=2 * OUT_ROW), :]
    return limit / jnp.sqrt(total_of(squares))


def tile_of(box, s):
    return jnp.concatenate([box[pl.ds(2 * s + c, B, stride=OUT_ROW), :] for c in range(2)], axis=1)


def shape_kernel(limit, chunks, box, left, right, moment, sent_hbm, shaped, sent, sems):
    clip = clip_of(limit, box)
    adam_sums, shaped_sums = [], []
    for s in range(SLOT_DEV):
        tile = tile_of(box, s) * clip
        half = dot(left[s], tile.astype(BF16)).astype(BF16)
        result = dot(half, right[s])
        shaped[s] = result
        square = tile * tile
        moment_new = 0.9 * moment[s] + 0.1 * square
        adam_sums.append(fold(square / moment_new))
        shaped_sums.append(fold(result * result))
    ratios = []
    for s in range(SLOT_DEV):
        adam_mean = total_of(adam_sums[s]) * (1.0 / (B * B))
        shaped_mean = total_of(shaped_sums[s]) * (1.0 / (B * B))
        ratios.append(jnp.sqrt(adam_mean) / jnp.sqrt(shaped_mean + 1e-06))
    rows = B // chunks
    out = []
    for k in range(chunks):
        for s in range(SLOT_DEV):
            result = shaped[s, k * rows : (k + 1) * rows, :] * ratios[s]
            for c in range(2):
                at = k * rows * BACK_ROW + 2 * s + c
                sent[pl.ds(at, rows, stride=BACK_ROW), :] = result[:, c * LANES : (c + 1) * LANES]
        part = pl.ds(k * rows * BACK_ROW, rows * BACK_ROW)
        out.append(started(sent.at[part], sent_hbm.at[part], sems.at[k]))
    for copy in out:
        copy.wait()


def stats_kernel(limit, box, left, right, moment, left_out, right_out, moment_out):
    clip = clip_of(limit, box)
    for s in range(SLOT_DEV):
        tile = tile_of(box, s) * clip
        moment_out[s] = 0.9 * moment[s] + 0.1 * (tile * tile)
        high = tile.astype(BF16)
        low = (tile - high.astype(F32)).astype(BF16)
        high_t, low_t = jnp.transpose(high), jnp.transpose(low)
        left_out[s] = 0.95 * left[s] + (dot(high, high_t) + (dot(high, low_t) + dot(low, high_t)))
        right_out[s] = 0.95 * right[s] + (dot(high_t, high) + (dot(high_t, low) + dot(low_t, high)))


def unpack_kernel(chunks, place, box, update_hbm, update, sems):
    groups = update.shape[0] // chunks
    out = []
    for k in range(chunks):

        def group(g, carry):
            for j in range(8):
                at = place[g * 8 + j]
                for q in range(4):
                    update[g, j : j + 1, q * LANES : (q + 1) * LANES] = box[
                        pl.ds(at + q // 2 * BACK_ROW + q % 2, 1), :
                    ]
            return carry

        lax.fori_loop(k * groups, (k + 1) * groups, group, 0)
        part = pl.ds(k * groups, groups)
        out.append(started(update.at[part], update_hbm.at[part], sems.at[k]))
    for copy in out:
        copy.wait()


def exchange(box):
    rows = box.reshape(box.shape[0], 1, LANES)
    rows = lax.all_to_all(rows, "shard", split_axis=0, concat_axis=0, tiled=True)
    return rows.reshape(box.shape)


def shards(grads, owner, left_stat, right_stat, left_root, right_root, moment):
    devices = lax.axis_size("shard")
    tiles, shard_len = grads.shape
    limit = math.sqrt(tiles * shard_len * devices)
    out_shape = jax.ShapeDtypeStruct((devices * 2 * OUT_ROW, LANES), F32)
    back_shape = jax.ShapeDtypeStruct((devices * 2 * BACK_ROW, LANES), F32)
    update_shape = jax.ShapeDtypeStruct((tiles // 8, 8, shard_len), F32)
    slots = left_stat.shape
    dma = pltpu.SemaphoreType.DMA

    outbox, place = call(
        functools.partial(pack_kernel, 4), [ANY, ANY], [VMEM, VMEM],
        [out_shape, jax.ShapeDtypeStruct((8, tiles), jnp.int32)],
        [pltpu.VMEM((1, tiles), jnp.int32), pltpu.VMEM(grads.shape, F32), dma((2,))],
        6 * tiles * devices * SLOT_DEV * shard_len, 16 * grads.size, 56,
    )(owner.reshape(1, tiles), grads)
    place = place[0]
    arrived = exchange(outbox)

    sent = call(
        functools.partial(shape_kernel, limit, 4), [VMEM] * 4, ANY, back_shape,
        [pltpu.VMEM(slots, F32), pltpu.VMEM(back_shape.shape, F32), dma((4,))],
        SLOT_DEV * 4 * B**3, SLOT_DEV * B * B * 16, 16,
    )(arrived, left_root, right_root, moment)
    returned = exchange(sent)

    left_new, right_new, moment_new = call(
        functools.partial(stats_kernel, limit), [VMEM] * 4, [VMEM] * 3, [jax.ShapeDtypeStruct(slots, F32)] * 3,
        [], SLOT_DEV * 12 * B**3, SLOT_DEV * B * B * 28, 32,
    )(arrived, left_stat, right_stat, moment)

    update = call(
        functools.partial(unpack_kernel, 3), [SMEM, VMEM], ANY, update_shape,
        [pltpu.VMEM(update_shape.shape, F32), dma((3,))], 2 * grads.size, 16 * grads.size, 8,
    )(place, returned)
    return (update.reshape(grads.shape), left_new, right_new, moment_new)


def solution(mesh):
    return jax.shard_map(
        shards,
        mesh=mesh,
        in_specs=(
            P(None, "shard"),
            P(),
            P("shard", None, None),
            P("shard", None, None),
            P("shard", None, None),
            P("shard", None, None),
            P("shard", None, None),
        ),
        out_specs=(
            P(None, "shard"),
            P("shard", None, None),
            P("shard", None, None),
            P("shard", None, None),
        ),
        check_vma=False,
    )
```

time: 175 us -> 91.3 us (0.52)
  blocking collectives: 104 us -> 43.4 us
  Pallas kernels: 0 us -> 14.7 us
  matrix products: 13.8 us -> 0 us
  other arithmetic: 13.3 us -> 0 us
  local copies, waits for them, and re-layouts: 16.8 us -> 6.8 us
    psum x1 -> x0, blocking collectives: 68.7 us -> none  [shards(): squares_all = lax.psum(jnp.sum(grads * grads), 'shard')]
    pallas_call x0 -> x4, Pallas kernels: none -> 14.7 us  [the longest x1 4.89 us: shards(): call(functools.partial(stats_kernel, limit), [VMEM] * 4, [VMEM] * 3, [jax...]
    dot_general x3 -> x0, matrix products: 13.8 us -> none  [the longest x1 6.56 us: shards(): jnp.einsum('sji,sjk->sik', blocks, blocks, precision=highest, preferred_e...]
    reshape x4 -> x0, local copies, waits for them, and re-layouts: 10.1 us -> none  [the longest x2 6.96 us: shards(): (shaped * graft_ratio[:, None, None]).reshape(slot_count, devices, shard_...]
    all_to_all x1, blocking collectives: 34.9 us -> 43.4 us  [exchange(): lax.all_to_all(rows, 'shard', split_axis=0, concat_axis=0, tiled=True)]
    unnamed x4 -> x14, local copies, waits for them, and re-layouts: 0.02 us -> 6.08 us
    reduce_sum x3 -> x0, other arithmetic: 5.63 us -> none  [the longest x1 3.45 us: shards(): jnp.mean(adam_step * adam_step, axis=(1, 2))]
    gather x1 -> x0, local copies, waits for them, and re-layouts: 4.23 us -> none  [shards(): update = gathered_rows[target]]
  transfers between devices with their start and end apart: 1 -> 1, of which waited for: 1 -> 1; matrix products, arithmetic and copies ran while one was open for 6% -> 1% of each run, Pallas kernels for 0% -> 5%
where the time goes in v2:
time: 91.3 us; the launch traced here: 90.9 us
  blocking collectives  43.4 us (48%)
  waiting for transfers between devices  19.8 us (22%)
  Pallas kernels  14.7 us (16%)
  local copies, waits for them, and re-layouts  6.8 us (7%)
  starting transfers between devices  5.57 us (6%)
    all_to_all x1, blocking collectives, exchange(): lax.all_to_all(rows, 'shard', split_axis=0, concat_axis=0, tiled=True)  43.4 us
    all_to_all x1, waiting for transfers between devices, exchange(): lax.all_to_all(rows, 'shard', split_axis=0, concat_axis=0, tiled=True)  19.8 us
    unnamed x14, local copies, waits for them, and re-layouts  6.08 us
    all_to_all x1, starting transfers between devices, exchange(): lax.all_to_all(rows, 'shard', split_axis=0, concat_axis=0, tiled=True)  5.57 us
    pallas_call x1, Pallas kernels, shards(): call(functools.partial(stats_kernel, limit), [VMEM] * 4, [VMEM] * 3, [jax...  4.89 us
    pallas_call x1, Pallas kernels, shards(): call(functools.partial(pack_kernel, 4), [ANY, ANY], [VMEM, VMEM], [out_sh...  4.09 us
    pallas_call x1, Pallas kernels, shards(): call(functools.partial(unpack_kernel, 3), [SMEM, VMEM], ANY, update_shape...  3.31 us
    pallas_call x1, Pallas kernels, shards(): call(functools.partial(shape_kernel, limit, 4), [VMEM] * 4, ANY, back_sha...  2.41 us
  transfers between devices with their start and end apart: 1, of which 1 were waited for; matrix products, arithmetic and copies ran while one was open for 1% of the time, Pallas kernels for 5%

profile of v2, /device:TPU:1, one launch (start us, length us, event | category | flops | bytes accessed | tf_op | source)
XLA Modules:
  0.0 90.9 jit_solution(6677824663267134577)
XLA Ops:
  0.6 4.1 %shard_map.102 = (f32[4352,128]{1,0:T(8,128)}, s32[8,384]{1,0:T(8,128)}) custom-call(s32[1,384]{1,0:T(1,128)} %bitcast.15, f32[384,512]{1,0:T(8,128)} %grads_hbm.1), custom_call_target="tpu_custom_call" | custom-call | flops 1207959552 | bytes 3145728 | tf_op jit(solution)/shard_map/pallas_call | solution.py:185
  4.7 0.0 copy-start.1
  4.7 0.0 copy-start.5
  4.8 0.0 copy-start.6
  4.8 43.4 %all_to_all.10 = f32[4352,1,128]{2,1,0:T(1,128)S(1)} all-to-all(f32[4352,1,128]{2,1,0:T(1,128)} %bitcast.13), channel_id=1, replica_groups=mesh['shard'=128] {'shard'}, dimensions={0} | all-to-all | bytes 4456448 | tf_op jit(solution)/shard_map/all_to_all | solution.py:171
  48.1 0.0 copy-done.1
  48.1 0.0 copy-done.5
  48.1 0.0 copy-done.6
  48.1 2.4 %shard_map.103 = f32[4096,128]{1,0:T(8,128)S(1)} custom-call(f32[4352,128]{1,0:T(8,128)S(1)} %bitcast.10, bf16[8,256,256]{2,1,0:T(8,128)(2,1)S(1)} %copy-done.5, bf16[8,256,256]{2,1,0:T(8,128)(2,1)S(1)} %copy-done.6, f32[8,256,256]{2,1,0:T(8,128)S(1)} %copy-done.1), custom_call_target="tpu_custom_call" | custom-call | flops 536870912 | bytes 8388608 | tf_op jit(solution)/shard_map/pallas_call | solution.py:194
  50.5 0.0 copy-start
  50.6 1.3 %copy-done = f32[4096,128]{1,0:T(8,128)} copy-done((f32[4096,128]{1,0:T(8,128)}, f32[4096,128]{1,0:T(8,128)S(1)}, u32[]{:S(2)}) %copy-start) | copy-done | bytes 2097176
  51.9 5.6 %all-to-all-start.1 = ((f32[4096,1,128]{2,1,0:T(1,128)}), f32[4096,1,128]{2,1,0:T(1,128)}, u32[]{:S(2)}, u32[]{:S(2)}) async-start(f32[4096,1,128]{2,1,0:T(1,128)} %bitcast.12), calls=%async_computation.1 | async-start | bytes 4194304 | tf_op jit(solution)/shard_map/all_to_all | solution.py:171
  57.4 0.7 slice_reduce_fusion.place
  58.2 0.0 copy-start.2
  58.2 1.6 %copy-done.2 = f32[8,256,256]{2,1,0:T(8,128)S(1)} copy-done((f32[8,256,256]{2,1,0:T(8,128)S(1)}, f32[8,256,256]{2,1,0:T(8,128)}, u32[]{:S(2)}) %copy-start.2) | copy-done | bytes 2097176
  59.7 0.0 copy-start.3
  59.7 1.6 %copy-done.3 = f32[8,256,256]{2,1,0:T(8,128)S(1)} copy-done((f32[8,256,256]{2,1,0:T(8,128)S(1)}, f32[8,256,256]{2,1,0:T(8,128)}, u32[]{:S(2)}) %copy-start.3) | copy-done | bytes 2097176
  61.3 0.0 copy-start.4
  61.3 1.6 %copy-done.4 = f32[8,256,256]{2,1,0:T(8,128)S(1)} copy-done((f32[8,256,256]{2,1,0:T(8,128)S(1)}, f32[8,256,256]{2,1,0:T(8,128)}, u32[]{:S(2)}) %copy-start.4) | copy-done | bytes 2097176
  62.9 4.9 %shard_map.105 = (f32[8,256,256]{2,1,0:T(8,128)}, f32[8,256,256]{2,1,0:T(8,128)}, f32[8,256,256]{2,1,0:T(8,128)}) custom-call(f32[4352,128]{1,0:T(8,128)S(1)} %bitcast.11, f32[8,256,256]{2,1,0:T(8,128)S(1)} %copy-done.3, f32[8,256,256]{2,1,0:T(8,128)S(1)} %copy-done.4, f32[8,256,256]{2,1,0:T(8,128)S(1)} %copy-done.2), custom_call_target="tpu_custom_call" | custom-call | flops 1610612736 | bytes 14680064 | tf_op jit(solution)/shard_map/pallas_call | solution.py:201
  67.8 19.8 %all-to-all-done.1 = f32[4096,1,128]{2,1,0:T(1,128)} async-done(((f32[4096,1,128]{2,1,0:T(1,128)}), f32[4096,1,128]{2,1,0:T(1,128)}, u32[]{:S(2)}, u32[]{:S(2)}) %all-to-all-start.1) | async-done | bytes 2097184 | tf_op jit(solution)/shard_map/all_to_all | solution.py:171
  87.6 3.3 %shard_map.104 = f32[48,8,512]{2,1,0:T(8,128)} custom-call(s32[384]{0:T(512)S(1)} %slice_reduce_fusion.place, f32[4096,128]{1,0:T(8,128)} %bitcast.6.box), custom_call_target="tpu_custom_call" | custom-call | flops 393216 | bytes 3145728 | tf_op jit(solution)/shard_map/pallas_call | solution.py:206
Async XLA Ops:
  4.7 43.4 %copy-start.1 = (f32[8,256,256]{2,1,0:T(8,128)S(1)}, f32[8,256,256]{2,1,0:T(8,128)}, u32[]{:S(2)}) copy-start(f32[8,256,256]{2,1,0:T(8,128)} %moment.3) | copy-start | bytes 6291460
  4.7 43.4 %copy-start.5 = (bf16[8,256,256]{2,1,0:T(8,128)(2,1)S(1)}, bf16[8,256,256]{2,1,0:T(8,128)(2,1)}, u32[]{:S(2)}) copy-start(bf16[8,256,256]{2,1,0:T(8,128)(2,1)} %left.2) | copy-start | bytes 3145732
  4.8 43.4 %copy-start.6 = (bf16[8,256,256]{2,1,0:T(8,128)(2,1)S(1)}, bf16[8,256,256]{2,1,0:T(8,128)(2,1)}, u32[]{:S(2)}) copy-start(bf16[8,256,256]{2,1,0:T(8,128)(2,1)} %right.2) | copy-start | bytes 3145732
  50.5 1.3 %copy-start = (f32[4096,128]{1,0:T(8,128)}, f32[4096,128]{1,0:T(8,128)S(1)}, u32[]{:S(2)}) copy-start(f32[4096,128]{1,0:T(8,128)S(1)} %shard_map.103) | copy-start | bytes 6291460
  51.9 35.8 %all-to-all-start.1 = ((f32[4096,1,128]{2,1,0:T(1,128)}), f32[4096,1,128]{2,1,0:T(1,128)}, u32[]{:S(2)}, u32[]{:S(2)}) async-start(f32[4096,1,128]{2,1,0:T(1,128)} %bitcast.12), calls=%async_computation.1 | async-start | bytes 4194304 | tf_op jit(solution)/shard_map/all_to_all | solution.py:171
  58.2 1.6 %copy-start.2 = (f32[8,256,256]{2,1,0:T(8,128)S(1)}, f32[8,256,256]{2,1,0:T(8,128)}, u32[]{:S(2)}) copy-start(f32[8,256,256]{2,1,0:T(8,128)} %moment.3) | copy-start | bytes 6291460
  59.7 1.6 %copy-start.3 = (f32[8,256,256]{2,1,0:T(8,128)S(1)}, f32[8,256,256]{2,1,0:T(8,128)}, u32[]{:S(2)}) copy-start(f32[8,256,256]{2,1,0:T(8,128)} %left.3) | copy-start | bytes 6291460
  61.3 1.6 %copy-start.4 = (f32[8,256,256]{2,1,0:T(8,128)S(1)}, f32[8,256,256]{2,1,0:T(8,128)}, u32[]{:S(2)}) copy-start(f32[8,256,256]{2,1,0:T(8,128)} %right.3) | copy-start | bytes 6291460

commit v3 on v2

--- a/solution.py
+++ b/solution.py
@@ -14,7 +14,7 @@
 OUT_ROW = 2 * SLOT_DEV + 1
 BACK_ROW = 2 * SLOT_DEV
 
-ANY = pl.BlockSpec(memory_space=pl.ANY)
+HBM = pl.BlockSpec(memory_space=pltpu.HBM)
 VMEM = pl.BlockSpec(memory_space=pltpu.VMEM)
 SMEM = pl.BlockSpec(memory_space=pltpu.SMEM)
 F32 = jnp.float32
@@ -39,12 +39,9 @@
     return copy
 
 
-def three_terms(x):
+def two_terms(x):
     high = x.astype(BF16)
-    rest = x - high.astype(F32)
-    middle = rest.astype(BF16)
-    low = (rest - middle.astype(F32)).astype(BF16)
-    return high, middle, low
+    return high, (x - high.astype(F32)).astype(BF16)
 
 
 def dot(a, b):
@@ -60,31 +57,35 @@
     return jnp.sum(jnp.sum(x, axis=0, keepdims=True), axis=1, keepdims=True)
 
 
-def pack_kernel(chunks, owner_hbm, grads_hbm, box, place_ref, owner, grads, sems):
+def pack_kernel(chunks, owner_hbm, grads_hbm, box, place_ref, owner, grads, chosen, sems):
     copies = [started(owner_hbm, owner, sems.at[0]), started(grads_hbm, grads, sems.at[1])]
     tiles = grads.shape[0]
     message = 2 * OUT_ROW
+    sub = lax.broadcasted_iota(jnp.int32, (tiles, tiles), 0)
+    lane = lax.broadcasted_iota(jnp.int32, (tiles, tiles), 1)
+    box[pl.ds(message - 1, LANES, stride=message), :] = jnp.zeros((LANES, LANES), F32)
     copies[0].wait()
     owner_row = owner[...].astype(F32)
     owner_col = jnp.transpose(jnp.broadcast_to(owner_row, (8, tiles)))[:, :1]
-    sub = lax.broadcasted_iota(jnp.int32, (tiles, tiles), 0)
-    lane = lax.broadcasted_iota(jnp.int32, (tiles, tiles), 1)
     earlier = (owner_col == owner_row) & (sub < lane)
     rank = jnp.sum(earlier.astype(F32), axis=0, keepdims=True)
-    place = rank * LANES + owner_row
     back = rank * 2 + owner_row * (2 * BACK_ROW)
     place_ref[...] = jnp.broadcast_to(back, (8, tiles)).astype(jnp.int32)
+    dests = LANES // chunks
+    rows = SLOT_DEV * dests
+    sub = lax.broadcasted_iota(jnp.int32, (dests, tiles), 0).astype(F32)
+    for k in range(chunks):
+        mine = sub == owner_row - float(k * dests)
+        for s in range(SLOT_DEV):
+            at = k * rows + s * dests
+            chosen[at : at + dests, :] = (mine & (rank == float(s))).astype(BF16)
     copies[1].wait()
     squares = jnp.sum(fold(jnp.square(grads[...])), axis=0, keepdims=True)
     box[pl.ds(OUT_ROW - 1, LANES, stride=message), :] = jnp.broadcast_to(squares, (LANES, LANES))
-    box[pl.ds(message - 1, LANES, stride=message), :] = jnp.zeros((LANES, LANES), F32)
-    terms = jnp.concatenate(three_terms(grads[...]), axis=0)
-    dests = LANES // chunks
-    sub = lax.broadcasted_iota(jnp.int32, (SLOT_DEV * dests, tiles), 0)
-    slots = (sub // dests * LANES + sub % dests).astype(F32)
-    for k in range(chunks):
-        chosen = (slots == place - float(k * dests)).astype(BF16)
-        sent = dot(jnp.concatenate([chosen] * 3, axis=1), terms)
+    terms = two_terms(grads[...])
+    for k in range(chunks):
+        taken = chosen[k * rows : (k + 1) * rows, :]
+        sent = dot(taken, terms[0]) + dot(taken, terms[1])
         for s in range(SLOT_DEV):
             for q in range(4):
                 at = k * dests * message + q // 2 * OUT_ROW + 2 * s + q % 2
@@ -176,37 +177,40 @@
     devices = lax.axis_size("shard")
     tiles, shard_len = grads.shape
     limit = math.sqrt(tiles * shard_len * devices)
-    out_shape = jax.ShapeDtypeStruct((devices * 2 * OUT_ROW, LANES), F32)
-    back_shape = jax.ShapeDtypeStruct((devices * 2 * BACK_ROW, LANES), F32)
-    update_shape = jax.ShapeDtypeStruct((tiles // 8, 8, shard_len), F32)
+    out_shape = (devices * 2 * OUT_ROW, LANES)
+    back_shape = (devices * 2 * BACK_ROW, LANES)
+    update_shape = (tiles // 8, 8, shard_len)
+    in_hbm = functools.partial(pltpu.with_memory_space_constraint, memory_space=pltpu.HBM)
+    in_vmem = functools.partial(pltpu.with_memory_space_constraint, memory_space=pltpu.VMEM)
     slots = left_stat.shape
     dma = pltpu.SemaphoreType.DMA
 
     outbox, place = call(
-        functools.partial(pack_kernel, 4), [ANY, ANY], [VMEM, VMEM],
-        [out_shape, jax.ShapeDtypeStruct((8, tiles), jnp.int32)],
-        [pltpu.VMEM((1, tiles), jnp.int32), pltpu.VMEM(grads.shape, F32), dma((2,))],
-        6 * tiles * devices * SLOT_DEV * shard_len, 16 * grads.size, 56,
-    )(owner.reshape(1, tiles), grads)
+        functools.partial(pack_kernel, 2), [HBM, HBM], [VMEM, VMEM],
+        [pltpu.VMEM(out_shape, F32), jax.ShapeDtypeStruct((8, tiles), jnp.int32)],
+        [pltpu.VMEM((1, tiles), jnp.int32), pltpu.VMEM(grads.shape, F32),
+         pltpu.VMEM((devices * SLOT_DEV, tiles), BF16), dma((2,))],
+        4 * tiles * devices * SLOT_DEV * shard_len, 16 * grads.size, 16,
+    )(in_hbm(owner.reshape(1, tiles)), in_hbm(grads))
     place = place[0]
     arrived = exchange(outbox)
 
     sent = call(
-        functools.partial(shape_kernel, limit, 4), [VMEM] * 4, ANY, back_shape,
-        [pltpu.VMEM(slots, F32), pltpu.VMEM(back_shape.shape, F32), dma((4,))],
+        functools.partial(shape_kernel, limit, 4), [VMEM] * 4, HBM, pltpu.HBM(back_shape, F32),
+        [pltpu.VMEM(slots, F32), pltpu.VMEM(back_shape, F32), dma((4,))],
         SLOT_DEV * 4 * B**3, SLOT_DEV * B * B * 16, 16,
     )(arrived, left_root, right_root, moment)
-    returned = exchange(sent)
+    returned = lax.all_to_all(sent, "shard", split_axis=0, concat_axis=0, tiled=True)
 
     left_new, right_new, moment_new = call(
         functools.partial(stats_kernel, limit), [VMEM] * 4, [VMEM] * 3, [jax.ShapeDtypeStruct(slots, F32)] * 3,
-        [], SLOT_DEV * 12 * B**3, SLOT_DEV * B * B * 28, 32,
+        [], SLOT_DEV * 12 * B**3, SLOT_DEV * B * B * 28, 20,
     )(arrived, left_stat, right_stat, moment)
 
     update = call(
-        functools.partial(unpack_kernel, 3), [SMEM, VMEM], ANY, update_shape,
-        [pltpu.VMEM(update_shape.shape, F32), dma((3,))], 2 * grads.size, 16 * grads.size, 8,
-    )(place, returned)
+        functools.partial(unpack_kernel, 3), [SMEM, VMEM], HBM, jax.ShapeDtypeStruct(update_shape, F32),
+        [pltpu.VMEM(update_shape, F32), dma((3,))], 2 * grads.size, 16 * grads.size, 8,
+    )(place, in_vmem(returned))
     return (update.reshape(grads.shape), left_new, right_new, moment_new)
 
 

time: 91.3 us -> 88.9 us (0.974)
  local copies, waits for them, and re-layouts: 6.8 us -> 4.8 us
    unnamed x14 -> x12, local copies, waits for them, and re-layouts: 6.08 us -> 4.79 us
  transfers between devices with their start and end apart: 1 -> 1, of which waited for: 1 -> 1; matrix products, arithmetic and copies ran while one was open for 1% -> 0% of each run, Pallas kernels for 5% -> 6%
where the time goes in v3:
time: 88.9 us; the launch traced here: 88.5 us
  blocking collectives  43.1 us (48%)
  waiting for transfers between devices  20.5 us (23%)
  Pallas kernels  13.9 us (16%)
  starting transfers between devices  5.58 us (6%)
  local copies, waits for them, and re-layouts  4.8 us (5%)
    all_to_all x1, blocking collectives, exchange(): lax.all_to_all(rows, 'shard', split_axis=0, concat_axis=0, tiled=True)  43.1 us
    all_to_all x1, waiting for transfers between devices, shards(): lax.all_to_all(sent, 'shard', split_axis=0, concat_axis=0, tiled=True)  20.5 us
    all_to_all x1, starting transfers between devices, shards(): lax.all_to_all(sent, 'shard', split_axis=0, concat_axis=0, tiled=True)  5.58 us
    pallas_call x1, Pallas kernels, shards(): call(functools.partial(stats_kernel, limit), [VMEM] * 4, [VMEM] * 3, [jax...  4.92 us
    unnamed x12, local copies, waits for them, and re-layouts  4.79 us
    pallas_call x1, Pallas kernels, shards(): call(functools.partial(unpack_kernel, 3), [SMEM, VMEM], HBM, jax.ShapeDty...  3.31 us
    pallas_call x1, Pallas kernels, shards(): call(functools.partial(shape_kernel, limit, 4), [VMEM] * 4, HBM, pltpu.HB...  3.13 us
    pallas_call x1, Pallas kernels, shards(): call(functools.partial(pack_kernel, 2), [HBM, HBM], [VMEM, VMEM], [pltpu....  2.5 us
  transfers between devices with their start and end apart: 1, of which 1 were waited for; matrix products, arithmetic and copies ran while one was open for 0% of the time, Pallas kernels for 6%

profile of v3, /device:TPU:1, one launch (start us, length us, event | category | flops | bytes accessed | tf_op | source)
XLA Modules:
  0.0 88.5 jit_solution(11312551029281894917)
XLA Ops:
  0.6 2.5 %shard_map.102 = (f32[4352,128]{1,0:T(8,128)S(1)}, s32[8,384]{1,0:T(8,128)S(1)}) custom-call(s32[1,384]{1,0:T(1,128)} %bitcast.13, f32[384,512]{1,0:T(8,128)} %grads_hbm.1), custom_call_target="tpu_custom_call" | custom-call | flops 805306368 | bytes 3145728 | tf_op jit(solution)/shard_map/pallas_call | solution.py:188
  3.1 0.0 copy-start
  3.1 0.0 copy-start.4
  3.2 0.0 copy-start.5
  3.2 43.1 %all_to_all.16 = f32[4352,1,128]{2,1,0:T(1,128)S(1)} all-to-all(f32[4352,1,128]{2,1,0:T(1,128)S(1)} %bitcast.10), channel_id=1, replica_groups=mesh['shard'=128] {'shard'}, dimensions={0} | all-to-all | bytes 4456448 | tf_op jit(solution)/shard_map/all_to_all | solution.py:172
  46.3 0.0 copy-done
  46.3 0.0 copy-done.4
  46.3 0.0 copy-done.5
  46.3 3.1 %shard_map.103 = f32[4096,128]{1,0:T(8,128)} custom-call(f32[4352,128]{1,0:T(8,128)S(1)} %bitcast.8, bf16[8,256,256]{2,1,0:T(8,128)(2,1)S(1)} %copy-done.4, bf16[8,256,256]{2,1,0:T(8,128)(2,1)S(1)} %copy-done.5, f32[8,256,256]{2,1,0:T(8,128)S(1)} %copy-done), custom_call_target="tpu_custom_call" | custom-call | flops 536870912 | bytes 8388608 | tf_op jit(solution)/shard_map/pallas_call | solution.py:198
  49.5 5.6 %all-to-all-start.1 = ((f32[128,32,128]{2,1,0:T(8,128)}), f32[128,32,128]{2,1,0:T(8,128)}, u32[]{:S(2)}, u32[]{:S(2)}) async-start(f32[128,32,128]{2,1,0:T(8,128)} %bitcast.11), calls=%async_computation.1 | async-start | bytes 4194304 | tf_op jit(solution)/shard_map/all_to_all | solution.py:203
  55.1 0.0 copy-start.1
  55.1 1.6 %copy-done.1 = f32[8,256,256]{2,1,0:T(8,128)S(1)} copy-done((f32[8,256,256]{2,1,0:T(8,128)S(1)}, f32[8,256,256]{2,1,0:T(8,128)}, u32[]{:S(2)}) %copy-start.1) | copy-done | bytes 2097176
  56.7 0.0 copy-start.2
  56.7 1.6 %copy-done.2 = f32[8,256,256]{2,1,0:T(8,128)S(1)} copy-done((f32[8,256,256]{2,1,0:T(8,128)S(1)}, f32[8,256,256]{2,1,0:T(8,128)}, u32[]{:S(2)}) %copy-start.2) | copy-done | bytes 2097176
  58.3 0.0 copy-start.3
  58.3 1.6 %copy-done.3 = f32[8,256,256]{2,1,0:T(8,128)S(1)} copy-done((f32[8,256,256]{2,1,0:T(8,128)S(1)}, f32[8,256,256]{2,1,0:T(8,128)}, u32[]{:S(2)}) %copy-start.3) | copy-done | bytes 2097176
  59.9 4.9 %shard_map.105 = (f32[8,256,256]{2,1,0:T(8,128)}, f32[8,256,256]{2,1,0:T(8,128)}, f32[8,256,256]{2,1,0:T(8,128)}) custom-call(f32[4352,128]{1,0:T(8,128)S(1)} %bitcast.9, f32[8,256,256]{2,1,0:T(8,128)S(1)} %copy-done.2, f32[8,256,256]{2,1,0:T(8,128)S(1)} %copy-done.3, f32[8,256,256]{2,1,0:T(8,128)S(1)} %copy-done.1), custom_call_target="tpu_custom_call" | custom-call | flops 1610612736 | bytes 14680064 | tf_op jit(solution)/shard_map/pallas_call | solution.py:205
  64.8 20.5 %all-to-all-done.1 = f32[128,32,128]{2,1,0:T(8,128)} async-done(((f32[128,32,128]{2,1,0:T(8,128)}), f32[128,32,128]{2,1,0:T(8,128)}, u32[]{:S(2)}, u32[]{:S(2)}) %all-to-all-start.1) | async-done | bytes 2097184 | tf_op jit(solution)/shard_map/all_to_all | solution.py:203
  85.2 3.3 %shard_map.104 = f32[48,8,512]{2,1,0:T(8,128)} custom-call(s32[384]{0:T(512)S(1)} %slice_reduce_fusion.place, f32[4096,128]{1,0:T(8,128)} %bitcast.5.box), custom_call_target="tpu_custom_call" | custom-call | flops 393216 | bytes 3145728 | tf_op jit(solution)/shard_map/pallas_call | solution.py:210
  (1 shorter events, 0.0 us)
Async XLA Ops:
  3.1 43.2 %copy-start = (f32[8,256,256]{2,1,0:T(8,128)S(1)}, f32[8,256,256]{2,1,0:T(8,128)}, u32[]{:S(2)}) copy-start(f32[8,256,256]{2,1,0:T(8,128)} %moment.3) | copy-start | bytes 6291460
  3.1 43.2 %copy-start.4 = (bf16[8,256,256]{2,1,0:T(8,128)(2,1)S(1)}, bf16[8,256,256]{2,1,0:T(8,128)(2,1)}, u32[]{:S(2)}) copy-start(bf16[8,256,256]{2,1,0:T(8,128)(2,1)} %left.2) | copy-start | bytes 3145732
  3.2 43.2 %copy-start.5 = (bf16[8,256,256]{2,1,0:T(8,128)(2,1)S(1)}, bf16[8,256,256]{2,1,0:T(8,128)(2,1)}, u32[]{:S(2)}) copy-start(bf16[8,256,256]{2,1,0:T(8,128)(2,1)} %right.2) | copy-start | bytes 3145732
  49.5 35.8 %all-to-all-start.1 = ((f32[128,32,128]{2,1,0:T(8,128)}), f32[128,32,128]{2,1,0:T(8,128)}, u32[]{:S(2)}, u32[]{:S(2)}) async-start(f32[128,32,128]{2,1,0:T(8,128)} %bitcast.11), calls=%async_computation.1 | async-start | bytes 4194304 | tf_op jit(solution)/shard_map/all_to_all | solution.py:203
  55.1 1.6 %copy-start.1 = (f32[8,256,256]{2,1,0:T(8,128)S(1)}, f32[8,256,256]{2,1,0:T(8,128)}, u32[]{:S(2)}) copy-start(f32[8,256,256]{2,1,0:T(8,128)} %moment.3) | copy-start | bytes 6291460
  56.7 1.6 %copy-start.2 = (f32[8,256,256]{2,1,0:T(8,128)S(1)}, f32[8,256,256]{2,1,0:T(8,128)}, u32[]{:S(2)}) copy-start(f32[8,256,256]{2,1,0:T(8,128)} %left.3) | copy-start | bytes 6291460
  58.3 1.6 %copy-start.3 = (f32[8,256,256]{2,1,0:T(8,128)S(1)}, f32[8,256,256]{2,1,0:T(8,128)}, u32[]{:S(2)}) copy-start(f32[8,256,256]{2,1,0:T(8,128)} %right.3) | copy-start | bytes 6291460

commit v4 on v3

--- a/solution.py
+++ b/solution.py
@@ -82,10 +82,10 @@
     copies[1].wait()
     squares = jnp.sum(fold(jnp.square(grads[...])), axis=0, keepdims=True)
     box[pl.ds(OUT_ROW - 1, LANES, stride=message), :] = jnp.broadcast_to(squares, (LANES, LANES))
-    terms = two_terms(grads[...])
+    terms = jnp.concatenate(two_terms(grads[...]), axis=0)
     for k in range(chunks):
         taken = chosen[k * rows : (k + 1) * rows, :]
-        sent = dot(taken, terms[0]) + dot(taken, terms[1])
+        sent = dot(jnp.concatenate([taken, taken], axis=1), terms)
         for s in range(SLOT_DEV):
             for q in range(4):
                 at = k * dests * message + q // 2 * OUT_ROW + 2 * s + q % 2
@@ -136,14 +136,14 @@
 
 def stats_kernel(limit, box, left, right, moment, left_out, right_out, moment_out):
     clip = clip_of(limit, box)
-    for s in range(SLOT_DEV):
-        tile = tile_of(box, s) * clip
-        moment_out[s] = 0.9 * moment[s] + 0.1 * (tile * tile)
-        high = tile.astype(BF16)
-        low = (tile - high.astype(F32)).astype(BF16)
-        high_t, low_t = jnp.transpose(high), jnp.transpose(low)
-        left_out[s] = 0.95 * left[s] + (dot(high, high_t) + (dot(high, low_t) + dot(low, high_t)))
-        right_out[s] = 0.95 * right[s] + (dot(high_t, high) + (dot(high_t, low) + dot(low_t, high)))
+    s = pl.program_id(0)
+    tile = jnp.concatenate([box[pl.ds(2 * s + c, B, stride=OUT_ROW), :] for c in range(2)], axis=1) * clip
+    moment_out[0] = 0.9 * moment[0] + 0.1 * (tile * tile)
+    high = tile.astype(BF16)
+    low = (tile - high.astype(F32)).astype(BF16)
+    high_t, low_t = jnp.transpose(high), jnp.transpose(low)
+    left_out[0] = 0.95 * left[0] + (dot(high, high_t) + (dot(high, low_t) + dot(low, high_t)))
+    right_out[0] = 0.95 * right[0] + (dot(high_t, high) + (dot(high_t, low) + dot(low_t, high)))
 
 
 def unpack_kernel(chunks, place, box, update_hbm, update, sems):
@@ -196,16 +196,22 @@
     arrived = exchange(outbox)
 
     sent = call(
-        functools.partial(shape_kernel, limit, 4), [VMEM] * 4, HBM, pltpu.HBM(back_shape, F32),
-        [pltpu.VMEM(slots, F32), pltpu.VMEM(back_shape, F32), dma((4,))],
+        functools.partial(shape_kernel, limit, 8), [VMEM] * 4, HBM, pltpu.HBM(back_shape, F32),
+        [pltpu.VMEM(slots, F32), pltpu.VMEM(back_shape, F32), dma((8,))],
         SLOT_DEV * 4 * B**3, SLOT_DEV * B * B * 16, 16,
     )(arrived, left_root, right_root, moment)
     returned = lax.all_to_all(sent, "shard", split_axis=0, concat_axis=0, tiled=True)
 
-    left_new, right_new, moment_new = call(
-        functools.partial(stats_kernel, limit), [VMEM] * 4, [VMEM] * 3, [jax.ShapeDtypeStruct(slots, F32)] * 3,
-        [], SLOT_DEV * 12 * B**3, SLOT_DEV * B * B * 28, 20,
-    )(arrived, left_stat, right_stat, moment)
+    slot = pl.BlockSpec((1, B, B), lambda s: (s, 0, 0))
+    left_new, right_new, moment_new = pl.pallas_call(
+        functools.partial(stats_kernel, limit),
+        grid=(SLOT_DEV,),
+        in_specs=[VMEM] + [slot] * 3,
+        out_specs=[slot] * 3,
+        out_shape=[pltpu.HBM(slots, F32)] * 3,
+        cost_estimate=pl.CostEstimate(flops=SLOT_DEV * 12 * B**3, bytes_accessed=SLOT_DEV * B * B * 28, transcendentals=0),
+        compiler_params=pltpu.CompilerParams(vmem_limit_bytes=8 * 1024 * 1024),
+    )(in_hbm(arrived), in_hbm(left_stat), in_hbm(right_stat), in_hbm(moment))
 
     update = call(
         functools.partial(unpack_kernel, 3), [SMEM, VMEM], HBM, jax.ShapeDtypeStruct(update_shape, F32),

time: 88.9 us -> 86.6 us (0.974)
  local copies, waits for them, and re-layouts: 4.8 us -> 0.04 us
  Pallas kernels: 13.9 us -> 17.6 us
  starting transfers between devices: 5.58 us -> 4.53 us
    pallas_call x2, Pallas kernels: 8.05 us -> 13.3 us  [the longest x1 10.3 us: shards(): pl.pallas_call(functools.partial(stats_kernel, limit), grid=(SLOT_DEV,),...]
    unnamed x12 -> x8, local copies, waits for them, and re-layouts: 4.79 us -> 0.02 us
    pallas_call x1, Pallas kernels: 3.31 us -> 2.14 us  [shards(): call(functools.partial(unpack_kernel, 3), [SMEM, VMEM], HBM, jax.ShapeDty...]
    all_to_all x1, starting transfers between devices: 5.58 us -> 4.53 us  [shards(): lax.all_to_all(sent, 'shard', split_axis=0, concat_axis=0, tiled=True)]
  transfers between devices with their start and end apart: 1 -> 1, of which waited for: 1 -> 1; matrix products, arithmetic and copies ran while one was open for 0% -> 0% of each run, Pallas kernels for 6% -> 12%
where the time goes in v4:
time: 86.6 us; the launch traced here: 86.2 us
  blocking collectives  43.1 us (50%)
  waiting for transfers between devices  20.2 us (23%)
  Pallas kernels  17.6 us (20%)
  starting transfers between devices  4.53 us (5%)
    all_to_all x1, blocking collectives, exchange(): lax.all_to_all(rows, 'shard', split_axis=0, concat_axis=0, tiled=True)  43.1 us
    all_to_all x1, waiting for transfers between devices, shards(): lax.all_to_all(sent, 'shard', split_axis=0, concat_axis=0, tiled=True)  20.2 us
    pallas_call x1, Pallas kernels, shards(): pl.pallas_call(functools.partial(stats_kernel, limit), grid=(SLOT_DEV,),...  10.3 us
    all_to_all x1, starting transfers between devices, shards(): lax.all_to_all(sent, 'shard', split_axis=0, concat_axis=0, tiled=True)  4.53 us
    pallas_call x1, Pallas kernels, shards(): call(functools.partial(shape_kernel, limit, 8), [VMEM] * 4, HBM, pltpu.HB...  2.99 us
    pallas_call x1, Pallas kernels, shards(): call(functools.partial(pack_kernel, 2), [HBM, HBM], [VMEM, VMEM], [pltpu....  2.19 us
    pallas_call x1, Pallas kernels, shards(): call(functools.partial(unpack_kernel, 3), [SMEM, VMEM], HBM, jax.ShapeDty...  2.14 us
  transfers between devices with their start and end apart: 1, of which 1 were waited for; matrix products, arithmetic and copies ran while one was open for 0% of the time, Pallas kernels for 12%

profile of v4, /device:TPU:1, one launch (start us, length us, event | category | flops | bytes accessed | tf_op | source)
XLA Modules:
  0.0 86.2 jit_solution(5906814673921994039)
XLA Ops:
  0.6 2.2 %shard_map.102 = (f32[4352,128]{1,0:T(8,128)S(1)}, s32[8,384]{1,0:T(8,128)S(1)}) custom-call(s32[1,384]{1,0:T(1,128)} %bitcast.14, f32[384,512]{1,0:T(8,128)} %grads_hbm.1), custom_call_target="tpu_custom_call" | custom-call | flops 805306368 | bytes 3145728 | tf_op jit(solution)/shard_map/pallas_call | solution.py:188
  2.8 0.0 copy-start.1
  2.8 0.0 copy-start.2
  2.9 0.0 copy-start.3
  2.9 43.1 %all_to_all.16 = f32[4352,1,128]{2,1,0:T(1,128)S(1)} all-to-all(f32[4352,1,128]{2,1,0:T(1,128)S(1)} %bitcast.11), channel_id=1, replica_groups=mesh['shard'=128] {'shard'}, dimensions={0} | all-to-all | bytes 4456448 | tf_op jit(solution)/shard_map/all_to_all | solution.py:172
  46.0 0.0 copy-start
  46.0 0.0 copy-done.1
  46.0 0.0 copy-done.2
  46.0 0.0 copy-done.3
  46.0 3.0 %shard_map.103 = f32[4096,128]{1,0:T(8,128)} custom-call(f32[4352,128]{1,0:T(8,128)S(1)} %bitcast.8, bf16[8,256,256]{2,1,0:T(8,128)(2,1)S(1)} %copy-done.2, bf16[8,256,256]{2,1,0:T(8,128)(2,1)S(1)} %copy-done.3, f32[8,256,256]{2,1,0:T(8,128)S(1)} %copy-done.1), custom_call_target="tpu_custom_call" | custom-call | flops 536870912 | bytes 8388608 | tf_op jit(solution)/shard_map/pallas_call | solution.py:198
  49.0 0.0 copy-done
  49.0 4.5 %all-to-all-start.1 = ((f32[128,32,128]{2,1,0:T(8,128)}), f32[128,32,128]{2,1,0:T(8,128)S(1)}, u32[]{:S(2)}, u32[]{:S(2)}) async-start(f32[128,32,128]{2,1,0:T(8,128)} %bitcast.12), calls=%async_computation.1 | async-start | bytes 4194304 | tf_op jit(solution)/shard_map/all_to_all | solution.py:203
  53.6 10.3 %shard_map.105 = (f32[8,256,256]{2,1,0:T(8,128)}, f32[8,256,256]{2,1,0:T(8,128)}, f32[8,256,256]{2,1,0:T(8,128)}) custom-call(f32[4352,128]{1,0:T(8,128)} %bitcast.9, f32[8,256,256]{2,1,0:T(8,128)} %left.3, f32[8,256,256]{2,1,0:T(8,128)} %right.3, f32[8,256,256]{2,1,0:T(8,128)} %moment.3), custom_call_target="tpu_custom_call" | custom-call | flops 1610612736 | bytes 14680064 | tf_op jit(solution)/shard_map/pallas_call | solution.py:206
  63.9 20.2 %all-to-all-done.1 = f32[128,32,128]{2,1,0:T(8,128)S(1)} async-done(((f32[128,32,128]{2,1,0:T(8,128)}), f32[128,32,128]{2,1,0:T(8,128)S(1)}, u32[]{:S(2)}, u32[]{:S(2)}) %all-to-all-start.1) | async-done | bytes 2097184 | tf_op jit(solution)/shard_map/all_to_all | solution.py:203
  84.1 2.1 %shard_map.104 = f32[48,8,512]{2,1,0:T(8,128)} custom-call(s32[384]{0:T(512)S(1)} %slice_reduce_fusion.place, f32[4096,128]{1,0:T(8,128)S(1)} %bitcast.10), custom_call_target="tpu_custom_call" | custom-call | flops 393216 | bytes 3145728 | tf_op jit(solution)/shard_map/pallas_call | solution.py:216
  (1 shorter events, 0.0 us)
Async XLA Ops:
  2.8 43.2 %copy-start.1 = (f32[8,256,256]{2,1,0:T(8,128)S(1)}, f32[8,256,256]{2,1,0:T(8,128)}, u32[]{:S(2)}) copy-start(f32[8,256,256]{2,1,0:T(8,128)} %moment.3) | copy-start | bytes 6291460
  2.8 43.2 %copy-start.2 = (bf16[8,256,256]{2,1,0:T(8,128)(2,1)S(1)}, bf16[8,256,256]{2,1,0:T(8,128)(2,1)}, u32[]{:S(2)}) copy-start(bf16[8,256,256]{2,1,0:T(8,128)(2,1)} %left.2) | copy-start | bytes 3145732
  2.9 43.2 %copy-start.3 = (bf16[8,256,256]{2,1,0:T(8,128)(2,1)S(1)}, bf16[8,256,256]{2,1,0:T(8,128)(2,1)}, u32[]{:S(2)}) copy-start(bf16[8,256,256]{2,1,0:T(8,128)(2,1)} %right.2) | copy-start | bytes 3145732
  46.0 3.0 %copy-start = (f32[4352,1,128]{2,1,0:T(1,128)}, f32[4352,1,128]{2,1,0:T(1,128)S(1)}, u32[]{:S(2)}) copy-start(f32[4352,1,128]{2,1,0:T(1,128)S(1)} %all_to_all.16) | copy-start | bytes 6684676
  49.0 35.1 %all-to-all-start.1 = ((f32[128,32,128]{2,1,0:T(8,128)}), f32[128,32,128]{2,1,0:T(8,128)S(1)}, u32[]{:S(2)}, u32[]{:S(2)}) async-start(f32[128,32,128]{2,1,0:T(8,128)} %bitcast.12), calls=%async_computation.1 | async-start | bytes 4194304 | tf_op jit(solution)/shard_map/all_to_all | solution.py:203

commit v5 on v4

--- a/solution.py
+++ b/solution.py
@@ -11,7 +11,8 @@
 B = 256
 SLOT_DEV = 8
 LANES = 128
-OUT_ROW = 2 * SLOT_DEV + 1
+OUT_ROW = 2 * SLOT_DEV
+OUT_MESSAGE = 2 * OUT_ROW + 1
 BACK_ROW = 2 * SLOT_DEV
 
 HBM = pl.BlockSpec(memory_space=pltpu.HBM)
@@ -60,10 +61,9 @@
 def pack_kernel(chunks, owner_hbm, grads_hbm, box, place_ref, owner, grads, chosen, sems):
     copies = [started(owner_hbm, owner, sems.at[0]), started(grads_hbm, grads, sems.at[1])]
     tiles = grads.shape[0]
-    message = 2 * OUT_ROW
+    message = OUT_MESSAGE
     sub = lax.broadcasted_iota(jnp.int32, (tiles, tiles), 0)
     lane = lax.broadcasted_iota(jnp.int32, (tiles, tiles), 1)
-    box[pl.ds(message - 1, LANES, stride=message), :] = jnp.zeros((LANES, LANES), F32)
     copies[0].wait()
     owner_row = owner[...].astype(F32)
     owner_col = jnp.transpose(jnp.broadcast_to(owner_row, (8, tiles)))[:, :1]
@@ -81,7 +81,7 @@
             chosen[at : at + dests, :] = (mine & (rank == float(s))).astype(BF16)
     copies[1].wait()
     squares = jnp.sum(fold(jnp.square(grads[...])), axis=0, keepdims=True)
-    box[pl.ds(OUT_ROW - 1, LANES, stride=message), :] = jnp.broadcast_to(squares, (LANES, LANES))
+    box[pl.ds(message - 1, LANES, stride=message), :] = jnp.broadcast_to(squares, (LANES, LANES))
     terms = jnp.concatenate(two_terms(grads[...]), axis=0)
     for k in range(chunks):
         taken = chosen[k * rows : (k + 1) * rows, :]
@@ -95,49 +95,57 @@
 
 
 def clip_of(limit, box):
-    squares = box[pl.ds(OUT_ROW - 1, LANES, stride=2 * OUT_ROW), :]
+    squares = box[pl.ds(OUT_MESSAGE - 1, LANES, stride=OUT_MESSAGE), :]
     return limit / jnp.sqrt(total_of(squares))
 
 
-def tile_of(box, s):
-    return jnp.concatenate([box[pl.ds(2 * s + c, B, stride=OUT_ROW), :] for c in range(2)], axis=1)
-
-
-def shape_kernel(limit, chunks, box, left, right, moment, sent_hbm, shaped, sent, sems):
+def tile_of(box, s, clip, rows):
+    for c in range(2):
+        for parity in range(2):
+            at = parity * OUT_ROW + 2 * s + c
+            rows[c, pl.ds(parity, LANES, stride=2), :] = box[pl.ds(at, LANES, stride=OUT_MESSAGE), :] * clip
+    return jnp.concatenate([rows[0], rows[1]], axis=1)
+
+
+def shape_kernel(limit, chunks, box, left, right, moment, sent_hbm, ordered, sent, sems):
     clip = clip_of(limit, box)
-    adam_sums, shaped_sums = [], []
+    rows_of = sent.reshape(B, BACK_ROW, LANES)
+    sums, out = [], []
+
+    def send(half, pieces):
+        ratios = []
+        for adam_sum, shaped_sum in sums[4 * half : 4 * half + 4]:
+            adam_mean = total_of(adam_sum) * (1.0 / (B * B))
+            shaped_mean = total_of(shaped_sum) * (1.0 / (B * B))
+            ratio = jnp.sqrt(adam_mean) / jnp.sqrt(shaped_mean + 1e-06)
+            ratios.append(jnp.broadcast_to(ratio, (2, LANES)))
+        ratios = jnp.concatenate(ratios, axis=0)
+        rows = B // pieces
+        for k in range(pieces):
+            part = (pl.ds(k * rows, rows), pl.ds(8 * half, 8))
+            rows_of[part] = rows_of[part] * ratios
+            out.append(started(rows_of.at[part], sent_hbm.at[part], sems.at[len(out)]))
+
     for s in range(SLOT_DEV):
-        tile = tile_of(box, s) * clip
+        tile = tile_of(box, s, clip, ordered.at[s])
         half = dot(left[s], tile.astype(BF16)).astype(BF16)
-        result = dot(half, right[s])
-        shaped[s] = result
+        shaped = dot(half, right[s])
+        for c in range(2):
+            sent[pl.ds(2 * s + c, B, stride=BACK_ROW), :] = shaped[:, c * LANES : (c + 1) * LANES]
         square = tile * tile
         moment_new = 0.9 * moment[s] + 0.1 * square
-        adam_sums.append(fold(square / moment_new))
-        shaped_sums.append(fold(result * result))
-    ratios = []
-    for s in range(SLOT_DEV):
-        adam_mean = total_of(adam_sums[s]) * (1.0 / (B * B))
-        shaped_mean = total_of(shaped_sums[s]) * (1.0 / (B * B))
-        ratios.append(jnp.sqrt(adam_mean) / jnp.sqrt(shaped_mean + 1e-06))
-    rows = B // chunks
-    out = []
-    for k in range(chunks):
-        for s in range(SLOT_DEV):
-            result = shaped[s, k * rows : (k + 1) * rows, :] * ratios[s]
-            for c in range(2):
-                at = k * rows * BACK_ROW + 2 * s + c
-                sent[pl.ds(at, rows, stride=BACK_ROW), :] = result[:, c * LANES : (c + 1) * LANES]
-        part = pl.ds(k * rows * BACK_ROW, rows * BACK_ROW)
-        out.append(started(sent.at[part], sent_hbm.at[part], sems.at[k]))
+        sums.append((fold(square / moment_new), fold(shaped * shaped)))
+        if s == 4:
+            send(0, chunks[0])
+    send(1, chunks[1])
     for copy in out:
         copy.wait()
 
 
-def stats_kernel(limit, box, left, right, moment, left_out, right_out, moment_out):
+def stats_kernel(limit, box, left, right, moment, left_out, right_out, moment_out, ordered):
     clip = clip_of(limit, box)
     s = pl.program_id(0)
-    tile = jnp.concatenate([box[pl.ds(2 * s + c, B, stride=OUT_ROW), :] for c in range(2)], axis=1) * clip
+    tile = tile_of(box, s, clip, ordered)
     moment_out[0] = 0.9 * moment[0] + 0.1 * (tile * tile)
     high = tile.astype(BF16)
     low = (tile - high.astype(F32)).astype(BF16)
@@ -148,19 +156,21 @@
 
 def unpack_kernel(chunks, place, box, update_hbm, update, sems):
     groups = update.shape[0] // chunks
+    unroll = 2
     out = []
     for k in range(chunks):
 
-        def group(g, carry):
-            for j in range(8):
-                at = place[g * 8 + j]
-                for q in range(4):
-                    update[g, j : j + 1, q * LANES : (q + 1) * LANES] = box[
-                        pl.ds(at + q // 2 * BACK_ROW + q % 2, 1), :
-                    ]
+        def group(step, carry):
+            for g in range(unroll):
+                for j in range(8):
+                    at = place[(step * unroll + g) * 8 + j]
+                    for q in range(4):
+                        update[step * unroll + g, j : j + 1, q * LANES : (q + 1) * LANES] = box[
+                            pl.ds(at + q // 2 * BACK_ROW + q % 2, 1), :
+                        ]
             return carry
 
-        lax.fori_loop(k * groups, (k + 1) * groups, group, 0)
+        lax.fori_loop(k * groups // unroll, (k + 1) * groups // unroll, group, 0)
         part = pl.ds(k * groups, groups)
         out.append(started(update.at[part], update_hbm.at[part], sems.at[k]))
     for copy in out:
@@ -177,7 +187,7 @@
     devices = lax.axis_size("shard")
     tiles, shard_len = grads.shape
     limit = math.sqrt(tiles * shard_len * devices)
-    out_shape = (devices * 2 * OUT_ROW, LANES)
+    out_shape = (devices * OUT_MESSAGE, LANES)
     back_shape = (devices * 2 * BACK_ROW, LANES)
     update_shape = (tiles // 8, 8, shard_len)
     in_hbm = functools.partial(pltpu.with_memory_space_constraint, memory_space=pltpu.HBM)
@@ -196,11 +206,11 @@
     arrived = exchange(outbox)
 
     sent = call(
-        functools.partial(shape_kernel, limit, 8), [VMEM] * 4, HBM, pltpu.HBM(back_shape, F32),
-        [pltpu.VMEM(slots, F32), pltpu.VMEM(back_shape, F32), dma((8,))],
+        functools.partial(shape_kernel, limit, (2, 8)), [VMEM] * 4, HBM, pltpu.HBM((B, BACK_ROW, LANES), F32),
+        [pltpu.VMEM((SLOT_DEV, 2, B, LANES), F32), pltpu.VMEM(back_shape, F32), dma((10,))],
         SLOT_DEV * 4 * B**3, SLOT_DEV * B * B * 16, 16,
     )(arrived, left_root, right_root, moment)
-    returned = lax.all_to_all(sent, "shard", split_axis=0, concat_axis=0, tiled=True)
+    returned = lax.all_to_all(sent.reshape(back_shape), "shard", split_axis=0, concat_axis=0, tiled=True)
 
     slot = pl.BlockSpec((1, B, B), lambda s: (s, 0, 0))
     left_new, right_new, moment_new = pl.pallas_call(
@@ -209,6 +219,7 @@
         in_specs=[VMEM] + [slot] * 3,
         out_specs=[slot] * 3,
         out_shape=[pltpu.HBM(slots, F32)] * 3,
+        scratch_shapes=[pltpu.VMEM((2, B, LANES), F32)],
         cost_estimate=pl.CostEstimate(flops=SLOT_DEV * 12 * B**3, bytes_accessed=SLOT_DEV * B * B * 28, transcendentals=0),
         compiler_params=pltpu.CompilerParams(vmem_limit_bytes=8 * 1024 * 1024),
     )(in_hbm(arrived), in_hbm(left_stat), in_hbm(right_stat), in_hbm(moment))

time: 86.6 us -> 85.9 us (level)
  no operation moved by 1% of the time
where the time goes in v5:
time: 85.9 us; the launch traced here: 85.5 us
  blocking collectives  42.4 us (49%)
  waiting for transfers between devices  20.2 us (24%)
  Pallas kernels  17.6 us (20%)
  starting transfers between devices  4.55 us (5%)
    all_to_all x1, blocking collectives, exchange(): lax.all_to_all(rows, 'shard', split_axis=0, concat_axis=0, tiled=True)  42.4 us
    all_to_all x1, waiting for transfers between devices, shards(): lax.all_to_all(sent.reshape(back_shape), 'shard', split_axis=0, concat_ax...  20.2 us
    pallas_call x1, Pallas kernels, shards(): pl.pallas_call(functools.partial(stats_kernel, limit), grid=(SLOT_DEV,),...  10.3 us
    all_to_all x1, starting transfers between devices, shards(): lax.all_to_all(sent.reshape(back_shape), 'shard', split_axis=0, concat_ax...  4.55 us
    pallas_call x1, Pallas kernels, shards(): call(functools.partial(shape_kernel, limit, (2, 8)), [VMEM] * 4, HBM, plt...  3.05 us
    pallas_call x1, Pallas kernels, shards(): call(functools.partial(pack_kernel, 2), [HBM, HBM], [VMEM, VMEM], [pltpu....  2.19 us
    pallas_call x1, Pallas kernels, shards(): call(functools.partial(unpack_kernel, 3), [SMEM, VMEM], HBM, jax.ShapeDty...  2.04 us
  transfers between devices with their start and end apart: 1, of which 1 were waited for; matrix products, arithmetic and copies ran while one was open for 0% of the time, Pallas kernels for 12%

profile of v5, /device:TPU:1, one launch (start us, length us, event | category | flops | bytes accessed | tf_op | source)
XLA Modules:
  0.0 85.5 jit_solution(8226035139308247422)
XLA Ops:
  0.6 2.2 %shard_map.102 = (f32[4224,128]{1,0:T(8,128)S(1)}, s32[8,384]{1,0:T(8,128)S(1)}) custom-call(s32[1,384]{1,0:T(1,128)} %bitcast.14, f32[384,512]{1,0:T(8,128)} %grads_hbm.1), custom_call_target="tpu_custom_call" | custom-call | flops 805306368 | bytes 3145728 | tf_op jit(solution)/shard_map/pallas_call | solution.py:198
  2.8 0.0 copy-start.1
  2.8 0.0 copy-start.2
  2.9 0.0 copy-start.3
  2.9 42.4 %all_to_all.16 = f32[4224,1,128]{2,1,0:T(1,128)S(1)} all-to-all(f32[4224,1,128]{2,1,0:T(1,128)S(1)} %bitcast.11), channel_id=1, replica_groups=mesh['shard'=128] {'shard'}, dimensions={0} | all-to-all | bytes 4325376 | tf_op jit(solution)/shard_map/all_to_all | solution.py:182
  45.3 0.0 copy-start
  45.3 0.0 copy-done.1
  45.3 0.0 copy-done.2
  45.3 0.0 copy-done.3
  45.3 3.0 %shard_map.103 = f32[256,16,128]{2,1,0:T(8,128)} custom-call(f32[4224,128]{1,0:T(8,128)S(1)} %bitcast.8, bf16[8,256,256]{2,1,0:T(8,128)(2,1)S(1)} %copy-done.2, bf16[8,256,256]{2,1,0:T(8,128)(2,1)S(1)} %copy-done.3, f32[8,256,256]{2,1,0:T(8,128)S(1)} %copy-done.1), custom_call_target="tpu_custom_call" | custom-call | flops 536870912 | bytes 8388608 | tf_op jit(solution)/shard_map/pallas_call | solution.py:208
  48.4 0.0 copy-done
  48.4 4.6 %all-to-all-start.1 = ((f32[128,32,128]{2,1,0:T(8,128)}), f32[128,32,128]{2,1,0:T(8,128)S(1)}, u32[]{:S(2)}, u32[]{:S(2)}) async-start(f32[128,32,128]{2,1,0:T(8,128)} %bitcast.12), calls=%async_computation.1 | async-start | bytes 4194304 | tf_op jit(solution)/shard_map/all_to_all | solution.py:213
  52.9 10.3 %shard_map.105 = (f32[8,256,256]{2,1,0:T(8,128)}, f32[8,256,256]{2,1,0:T(8,128)}, f32[8,256,256]{2,1,0:T(8,128)}) custom-call(f32[4224,128]{1,0:T(8,128)} %bitcast.9, f32[8,256,256]{2,1,0:T(8,128)} %left.3, f32[8,256,256]{2,1,0:T(8,128)} %right.3, f32[8,256,256]{2,1,0:T(8,128)} %moment.3), custom_call_target="tpu_custom_call" | custom-call | flops 1610612736 | bytes 14680064 | tf_op jit(solution)/shard_map/pallas_call | solution.py:216
  63.3 20.2 %all-to-all-done.1 = f32[128,32,128]{2,1,0:T(8,128)S(1)} async-done(((f32[128,32,128]{2,1,0:T(8,128)}), f32[128,32,128]{2,1,0:T(8,128)S(1)}, u32[]{:S(2)}, u32[]{:S(2)}) %all-to-all-start.1) | async-done | bytes 2097184 | tf_op jit(solution)/shard_map/all_to_all | solution.py:213
  83.5 2.0 %shard_map.104 = f32[48,8,512]{2,1,0:T(8,128)} custom-call(s32[384]{0:T(512)S(1)} %slice_reduce_fusion.place, f32[4096,128]{1,0:T(8,128)S(1)} %bitcast.10), custom_call_target="tpu_custom_call" | custom-call | flops 393216 | bytes 3145728 | tf_op jit(solution)/shard_map/pallas_call | solution.py:227
  (1 shorter events, 0.0 us)
Async XLA Ops:
  2.8 42.5 %copy-start.1 = (f32[8,256,256]{2,1,0:T(8,128)S(1)}, f32[8,256,256]{2,1,0:T(8,128)}, u32[]{:S(2)}) copy-start(f32[8,256,256]{2,1,0:T(8,128)} %moment.3) | copy-start | bytes 6291460
  2.8 42.4 %copy-start.2 = (bf16[8,256,256]{2,1,0:T(8,128)(2,1)S(1)}, bf16[8,256,256]{2,1,0:T(8,128)(2,1)}, u32[]{:S(2)}) copy-start(bf16[8,256,256]{2,1,0:T(8,128)(2,1)} %left.2) | copy-start | bytes 3145732
  2.9 42.4 %copy-start.3 = (bf16[8,256,256]{2,1,0:T(8,128)(2,1)S(1)}, bf16[8,256,256]{2,1,0:T(8,128)(2,1)}, u32[]{:S(2)}) copy-start(bf16[8,256,256]{2,1,0:T(8,128)(2,1)} %right.2) | copy-start | bytes 3145732
  45.3 3.1 %copy-start = (f32[4224,1,128]{2,1,0:T(1,128)}, f32[4224,1,128]{2,1,0:T(1,128)S(1)}, u32[]{:S(2)}) copy-start(f32[4224,1,128]{2,1,0:T(1,128)S(1)} %all_to_all.16) | copy-start | bytes 6488068
  48.4 35.1 %all-to-all-start.1 = ((f32[128,32,128]{2,1,0:T(8,128)}), f32[128,32,128]{2,1,0:T(8,128)S(1)}, u32[]{:S(2)}, u32[]{:S(2)}) async-start(f32[128,32,128]{2,1,0:T(8,128)} %bitcast.12), calls=%async_computation.1 | async-start | bytes 4194304 | tf_op jit(solution)/shard_map/all_to_all | solution.py:213

commit v6 on v5

--- a/solution.py
+++ b/solution.py
@@ -154,25 +154,25 @@
     right_out[0] = 0.95 * right[0] + (dot(high_t, high) + (dot(high_t, low) + dot(low_t, high)))
 
 
-def unpack_kernel(chunks, place, box, update_hbm, update, sems):
-    groups = update.shape[0] // chunks
-    unroll = 2
-    out = []
-    for k in range(chunks):
-
-        def group(step, carry):
+def unpack_kernel(sizes, unroll, place, box, update_hbm, update, sems):
+    first, out = 0, []
+    for k, size in enumerate(sizes):
+
+        def group(step, carry, first=first):
             for g in range(unroll):
-                for j in range(8):
-                    at = place[(step * unroll + g) * 8 + j]
-                    for q in range(4):
-                        update[step * unroll + g, j : j + 1, q * LANES : (q + 1) * LANES] = box[
-                            pl.ds(at + q // 2 * BACK_ROW + q % 2, 1), :
-                        ]
+                at_group = first + step * unroll + g
+                rows = [place[at_group * 8 + j] for j in range(8)]
+                for q in range(4):
+                    at = q // 2 * BACK_ROW + q % 2
+                    update[at_group, :, q * LANES : (q + 1) * LANES] = jnp.concatenate(
+                        [box[pl.ds(row + at, 1), :] for row in rows], axis=0
+                    )
             return carry
 
-        lax.fori_loop(k * groups // unroll, (k + 1) * groups // unroll, group, 0)
-        part = pl.ds(k * groups, groups)
+        lax.fori_loop(0, size // unroll, group, 0)
+        part = pl.ds(first, size)
         out.append(started(update.at[part], update_hbm.at[part], sems.at[k]))
+        first += size
     for copy in out:
         copy.wait()
 
@@ -225,7 +225,7 @@
     )(in_hbm(arrived), in_hbm(left_stat), in_hbm(right_stat), in_hbm(moment))
 
     update = call(
-        functools.partial(unpack_kernel, 3), [SMEM, VMEM], HBM, jax.ShapeDtypeStruct(update_shape, F32),
+        functools.partial(unpack_kernel, (24, 16, 8), 4), [SMEM, VMEM], HBM, jax.ShapeDtypeStruct(update_shape, F32),
         [pltpu.VMEM(update_shape, F32), dma((3,))], 2 * grads.size, 16 * grads.size, 8,
     )(place, in_vmem(returned))
     return (update.reshape(grads.shape), left_new, right_new, moment_new)

time: 85.9 us -> 85.7 us (level)
  no operation moved by 1% of the time
where the time goes in v6:
time: 85.7 us; the launch traced here: 85.3 us
  blocking collectives  42.4 us (49%)
  waiting for transfers between devices  20.2 us (24%)
  Pallas kernels  17.4 us (20%)
  starting transfers between devices  4.55 us (5%)
    all_to_all x1, blocking collectives, exchange(): lax.all_to_all(rows, 'shard', split_axis=0, concat_axis=0, tiled=True)  42.4 us
    all_to_all x1, waiting for transfers between devices, shards(): lax.all_to_all(sent.reshape(back_shape), 'shard', split_axis=0, concat_ax...  20.2 us
    pallas_call x1, Pallas kernels, shards(): pl.pallas_call(functools.partial(stats_kernel, limit), grid=(SLOT_DEV,),...  10.3 us
    all_to_all x1, starting transfers between devices, shards(): lax.all_to_all(sent.reshape(back_shape), 'shard', split_axis=0, concat_ax...  4.55 us
    pallas_call x1, Pallas kernels, shards(): call(functools.partial(shape_kernel, limit, (2, 8)), [VMEM] * 4, HBM, plt...  3.05 us
    pallas_call x1, Pallas kernels, shards(): call(functools.partial(pack_kernel, 2), [HBM, HBM], [VMEM, VMEM], [pltpu....  2.19 us
    pallas_call x1, Pallas kernels, shards(): call(functools.partial(unpack_kernel, (24, 16, 8), 4), [SMEM, VMEM], HBM,...  1.84 us
  transfers between devices with their start and end apart: 1, of which 1 were waited for; matrix products, arithmetic and copies ran while one was open for 0% of the time, Pallas kernels for 12%

profile of v6, /device:TPU:1, one launch (start us, length us, event | category | flops | bytes accessed | tf_op | source)
XLA Modules:
  0.0 85.3 jit_solution(10436768095605435280)
XLA Ops:
  0.6 2.2 %shard_map.102 = (f32[4224,128]{1,0:T(8,128)S(1)}, s32[8,384]{1,0:T(8,128)S(1)}) custom-call(s32[1,384]{1,0:T(1,128)} %bitcast.14, f32[384,512]{1,0:T(8,128)} %grads_hbm.1), custom_call_target="tpu_custom_call" | custom-call | flops 805306368 | bytes 3145728 | tf_op jit(solution)/shard_map/pallas_call | solution.py:198
  2.8 0.0 copy-start.1
  2.8 0.0 copy-start.2
  2.9 0.0 copy-start.3
  2.9 42.4 %all_to_all.16 = f32[4224,1,128]{2,1,0:T(1,128)S(1)} all-to-all(f32[4224,1,128]{2,1,0:T(1,128)S(1)} %bitcast.11), channel_id=1, replica_groups=mesh['shard'=128] {'shard'}, dimensions={0} | all-to-all | bytes 4325376 | tf_op jit(solution)/shard_map/all_to_all | solution.py:182
  45.3 0.0 copy-start
  45.3 0.0 copy-done.1
  45.3 0.0 copy-done.2
  45.3 0.0 copy-done.3
  45.3 3.0 %shard_map.103 = f32[256,16,128]{2,1,0:T(8,128)} custom-call(f32[4224,128]{1,0:T(8,128)S(1)} %bitcast.8, bf16[8,256,256]{2,1,0:T(8,128)(2,1)S(1)} %copy-done.2, bf16[8,256,256]{2,1,0:T(8,128)(2,1)S(1)} %copy-done.3, f32[8,256,256]{2,1,0:T(8,128)S(1)} %copy-done.1), custom_call_target="tpu_custom_call" | custom-call | flops 536870912 | bytes 8388608 | tf_op jit(solution)/shard_map/pallas_call | solution.py:208
  48.4 0.0 copy-done
  48.4 4.6 %all-to-all-start.1 = ((f32[128,32,128]{2,1,0:T(8,128)}), f32[128,32,128]{2,1,0:T(8,128)S(1)}, u32[]{:S(2)}, u32[]{:S(2)}) async-start(f32[128,32,128]{2,1,0:T(8,128)} %bitcast.12), calls=%async_computation.1 | async-start | bytes 4194304 | tf_op jit(solution)/shard_map/all_to_all | solution.py:213
  52.9 10.3 %shard_map.105 = (f32[8,256,256]{2,1,0:T(8,128)}, f32[8,256,256]{2,1,0:T(8,128)}, f32[8,256,256]{2,1,0:T(8,128)}) custom-call(f32[4224,128]{1,0:T(8,128)} %bitcast.9, f32[8,256,256]{2,1,0:T(8,128)} %left.3, f32[8,256,256]{2,1,0:T(8,128)} %right.3, f32[8,256,256]{2,1,0:T(8,128)} %moment.3), custom_call_target="tpu_custom_call" | custom-call | flops 1610612736 | bytes 14680064 | tf_op jit(solution)/shard_map/pallas_call | solution.py:216
  63.3 20.2 %all-to-all-done.1 = f32[128,32,128]{2,1,0:T(8,128)S(1)} async-done(((f32[128,32,128]{2,1,0:T(8,128)}), f32[128,32,128]{2,1,0:T(8,128)S(1)}, u32[]{:S(2)}, u32[]{:S(2)}) %all-to-all-start.1) | async-done | bytes 2097184 | tf_op jit(solution)/shard_map/all_to_all | solution.py:213
  83.5 1.8 %shard_map.104 = f32[48,8,512]{2,1,0:T(8,128)} custom-call(s32[384]{0:T(512)S(1)} %slice_reduce_fusion.place, f32[4096,128]{1,0:T(8,128)S(1)} %bitcast.10), custom_call_target="tpu_custom_call" | custom-call | flops 393216 | bytes 3145728 | tf_op jit(solution)/shard_map/pallas_call | solution.py:227
  (1 shorter events, 0.0 us)
Async XLA Ops:
  2.8 42.5 %copy-start.1 = (f32[8,256,256]{2,1,0:T(8,128)S(1)}, f32[8,256,256]{2,1,0:T(8,128)}, u32[]{:S(2)}) copy-start(f32[8,256,256]{2,1,0:T(8,128)} %moment.3) | copy-start | bytes 6291460
  2.8 42.4 %copy-start.2 = (bf16[8,256,256]{2,1,0:T(8,128)(2,1)S(1)}, bf16[8,256,256]{2,1,0:T(8,128)(2,1)}, u32[]{:S(2)}) copy-start(bf16[8,256,256]{2,1,0:T(8,128)(2,1)} %left.2) | copy-start | bytes 3145732
  2.9 42.4 %copy-start.3 = (bf16[8,256,256]{2,1,0:T(8,128)(2,1)S(1)}, bf16[8,256,256]{2,1,0:T(8,128)(2,1)}, u32[]{:S(2)}) copy-start(bf16[8,256,256]{2,1,0:T(8,128)(2,1)} %right.2) | copy-start | bytes 3145732
  45.3 3.1 %copy-start = (f32[4224,1,128]{2,1,0:T(1,128)}, f32[4224,1,128]{2,1,0:T(1,128)S(1)}, u32[]{:S(2)}) copy-start(f32[4224,1,128]{2,1,0:T(1,128)S(1)} %all_to_all.16) | copy-start | bytes 6488068
  48.4 35.1 %all-to-all-start.1 = ((f32[128,32,128]{2,1,0:T(8,128)}), f32[128,32,128]{2,1,0:T(8,128)S(1)}, u32[]{:S(2)}, u32[]{:S(2)}) async-start(f32[128,32,128]{2,1,0:T(8,128)} %bitcast.12), calls=%async_computation.1 | async-start | bytes 4194304 | tf_op jit(solution)/shard_map/all_to_all | solution.py:213

commit v7 on v6

--- a/solution.py
+++ b/solution.py
@@ -14,6 +14,7 @@
 OUT_ROW = 2 * SLOT_DEV
 OUT_MESSAGE = 2 * OUT_ROW + 1
 BACK_ROW = 2 * SLOT_DEV
+ROOM_ROW = 3 * SLOT_DEV
 
 HBM = pl.BlockSpec(memory_space=pltpu.HBM)
 VMEM = pl.BlockSpec(memory_space=pltpu.VMEM)
@@ -109,7 +110,7 @@
 
 def shape_kernel(limit, chunks, box, left, right, moment, sent_hbm, ordered, sent, sems):
     clip = clip_of(limit, box)
-    rows_of = sent.reshape(B, BACK_ROW, LANES)
+    rows_of = sent.reshape(B, ROOM_ROW, LANES)
     sums, out = [], []
 
     def send(half, pieces):
@@ -127,14 +128,15 @@
             out.append(started(rows_of.at[part], sent_hbm.at[part], sems.at[len(out)]))
 
     for s in range(SLOT_DEV):
-        tile = tile_of(box, s, clip, ordered.at[s])
+        tile = tile_of(box, s, clip, ordered.at[s % 2])
+        square = tile * tile
+        moment_new = 0.9 * moment[s] + 0.1 * square
+        adam_sum = fold(square / moment_new)
         half = dot(left[s], tile.astype(BF16)).astype(BF16)
         shaped = dot(half, right[s])
         for c in range(2):
-            sent[pl.ds(2 * s + c, B, stride=BACK_ROW), :] = shaped[:, c * LANES : (c + 1) * LANES]
-        square = tile * tile
-        moment_new = 0.9 * moment[s] + 0.1 * square
-        sums.append((fold(square / moment_new), fold(shaped * shaped)))
+            sent[pl.ds(2 * s + c, B, stride=ROOM_ROW), :] = shaped[:, c * LANES : (c + 1) * LANES]
+        sums.append((adam_sum, fold(shaped * shaped)))
         if s == 4:
             send(0, chunks[0])
     send(1, chunks[1])
@@ -206,8 +208,8 @@
     arrived = exchange(outbox)
 
     sent = call(
-        functools.partial(shape_kernel, limit, (2, 8)), [VMEM] * 4, HBM, pltpu.HBM((B, BACK_ROW, LANES), F32),
-        [pltpu.VMEM((SLOT_DEV, 2, B, LANES), F32), pltpu.VMEM(back_shape, F32), dma((10,))],
+        functools.partial(shape_kernel, limit, (2, 4)), [VMEM] * 4, HBM, pltpu.HBM((B, BACK_ROW, LANES), F32),
+        [pltpu.VMEM((2, 2, B, LANES), F32), pltpu.VMEM((B * ROOM_ROW, LANES), F32), dma((6,))],
         SLOT_DEV * 4 * B**3, SLOT_DEV * B * B * 16, 16,
     )(arrived, left_root, right_root, moment)
     returned = lax.all_to_all(sent.reshape(back_shape), "shard", split_axis=0, concat_axis=0, tiled=True)

time: 85.7 us -> 85.2 us (level)
  no operation moved by 1% of the time
where the time goes in v7:
time: 85.2 us; the launch traced here: 84.9 us
  blocking collectives  42.4 us (50%)
  waiting for transfers between devices  20.2 us (24%)
  Pallas kernels  17 us (20%)
  starting transfers between devices  4.55 us (5%)
    all_to_all x1, blocking collectives, exchange(): lax.all_to_all(rows, 'shard', split_axis=0, concat_axis=0, tiled=True)  42.4 us
    all_to_all x1, waiting for transfers between devices, shards(): lax.all_to_all(sent.reshape(back_shape), 'shard', split_axis=0, concat_ax...  20.2 us
    pallas_call x1, Pallas kernels, shards(): pl.pallas_call(functools.partial(stats_kernel, limit), grid=(SLOT_DEV,),...  10.3 us
    all_to_all x1, starting transfers between devices, shards(): lax.all_to_all(sent.reshape(back_shape), 'shard', split_axis=0, concat_ax...  4.55 us
    pallas_call x1, Pallas kernels, shards(): call(functools.partial(shape_kernel, limit, (2, 4)), [VMEM] * 4, HBM, plt...  2.61 us
    pallas_call x1, Pallas kernels, shards(): call(functools.partial(pack_kernel, 2), [HBM, HBM], [VMEM, VMEM], [pltpu....  2.19 us
    pallas_call x1, Pallas kernels, shards(): call(functools.partial(unpack_kernel, (24, 16, 8), 4), [SMEM, VMEM], HBM,...  1.84 us
  transfers between devices with their start and end apart: 1, of which 1 were waited for; matrix products, arithmetic and copies ran while one was open for 0% of the time, Pallas kernels for 12%

profile of v7, /device:TPU:1, one launch (start us, length us, event | category | flops | bytes accessed | tf_op | source)
XLA Modules:
  0.0 84.9 jit_solution(4306807075186127790)
XLA Ops:
  0.6 2.2 %shard_map.102 = (f32[4224,128]{1,0:T(8,128)S(1)}, s32[8,384]{1,0:T(8,128)S(1)}) custom-call(s32[1,384]{1,0:T(1,128)} %bitcast.14, f32[384,512]{1,0:T(8,128)} %grads_hbm.1), custom_call_target="tpu_custom_call" | custom-call | flops 805306368 | bytes 3145728 | tf_op jit(solution)/shard_map/pallas_call | solution.py:200
  2.8 0.0 copy-start.1
  2.8 0.0 copy-start.2
  2.9 0.0 copy-start.3
  2.9 42.4 %all_to_all.16 = f32[4224,1,128]{2,1,0:T(1,128)S(1)} all-to-all(f32[4224,1,128]{2,1,0:T(1,128)S(1)} %bitcast.11), channel_id=1, replica_groups=mesh['shard'=128] {'shard'}, dimensions={0} | all-to-all | bytes 4325376 | tf_op jit(solution)/shard_map/all_to_all | solution.py:184
  45.3 0.0 copy-start
  45.3 0.0 copy-done.1
  45.3 0.0 copy-done.2
  45.3 0.0 copy-done.3
  45.3 2.6 %shard_map.103 = f32[256,16,128]{2,1,0:T(8,128)} custom-call(f32[4224,128]{1,0:T(8,128)S(1)} %bitcast.8, bf16[8,256,256]{2,1,0:T(8,128)(2,1)S(1)} %copy-done.2, bf16[8,256,256]{2,1,0:T(8,128)(2,1)S(1)} %copy-done.3, f32[8,256,256]{2,1,0:T(8,128)S(1)} %copy-done.1), custom_call_target="tpu_custom_call" | custom-call | flops 536870912 | bytes 8388608 | tf_op jit(solution)/shard_map/pallas_call | solution.py:210
  47.9 0.0 copy-done
  47.9 4.6 %all-to-all-start.1 = ((f32[128,32,128]{2,1,0:T(8,128)}), f32[128,32,128]{2,1,0:T(8,128)S(1)}, u32[]{:S(2)}, u32[]{:S(2)}) async-start(f32[128,32,128]{2,1,0:T(8,128)} %bitcast.12), calls=%async_computation.1 | async-start | bytes 4194304 | tf_op jit(solution)/shard_map/all_to_all | solution.py:215
  52.5 10.3 %shard_map.105 = (f32[8,256,256]{2,1,0:T(8,128)}, f32[8,256,256]{2,1,0:T(8,128)}, f32[8,256,256]{2,1,0:T(8,128)}) custom-call(f32[4224,128]{1,0:T(8,128)} %bitcast.9, f32[8,256,256]{2,1,0:T(8,128)} %left.3, f32[8,256,256]{2,1,0:T(8,128)} %right.3, f32[8,256,256]{2,1,0:T(8,128)} %moment.3), custom_call_target="tpu_custom_call" | custom-call | flops 1610612736 | bytes 14680064 | tf_op jit(solution)/shard_map/pallas_call | solution.py:218
  62.8 20.2 %all-to-all-done.1 = f32[128,32,128]{2,1,0:T(8,128)S(1)} async-done(((f32[128,32,128]{2,1,0:T(8,128)}), f32[128,32,128]{2,1,0:T(8,128)S(1)}, u32[]{:S(2)}, u32[]{:S(2)}) %all-to-all-start.1) | async-done | bytes 2097184 | tf_op jit(solution)/shard_map/all_to_all | solution.py:215
  83.0 1.8 %shard_map.104 = f32[48,8,512]{2,1,0:T(8,128)} custom-call(s32[384]{0:T(512)S(1)} %slice_reduce_fusion.place, f32[4096,128]{1,0:T(8,128)S(1)} %bitcast.10), custom_call_target="tpu_custom_call" | custom-call | flops 393216 | bytes 3145728 | tf_op jit(solution)/shard_map/pallas_call | solution.py:229
  (1 shorter events, 0.0 us)
Async XLA Ops:
  2.8 42.5 %copy-start.1 = (f32[8,256,256]{2,1,0:T(8,128)S(1)}, f32[8,256,256]{2,1,0:T(8,128)}, u32[]{:S(2)}) copy-start(f32[8,256,256]{2,1,0:T(8,128)} %moment.3) | copy-start | bytes 6291460
  2.8 42.4 %copy-start.2 = (bf16[8,256,256]{2,1,0:T(8,128)(2,1)S(1)}, bf16[8,256,256]{2,1,0:T(8,128)(2,1)}, u32[]{:S(2)}) copy-start(bf16[8,256,256]{2,1,0:T(8,128)(2,1)} %left.2) | copy-start | bytes 3145732
  2.9 42.4 %copy-start.3 = (bf16[8,256,256]{2,1,0:T(8,128)(2,1)S(1)}, bf16[8,256,256]{2,1,0:T(8,128)(2,1)}, u32[]{:S(2)}) copy-start(bf16[8,256,256]{2,1,0:T(8,128)(2,1)} %right.2) | copy-start | bytes 3145732
  45.3 2.6 %copy-start = (f32[4224,1,128]{2,1,0:T(1,128)}, f32[4224,1,128]{2,1,0:T(1,128)S(1)}, u32[]{:S(2)}) copy-start(f32[4224,1,128]{2,1,0:T(1,128)S(1)} %all_to_all.16) | copy-start | bytes 6488068
  47.9 35.1 %all-to-all-start.1 = ((f32[128,32,128]{2,1,0:T(8,128)}), f32[128,32,128]{2,1,0:T(8,128)S(1)}, u32[]{:S(2)}, u32[]{:S(2)}) async-start(f32[128,32,128]{2,1,0:T(8,128)} %bitcast.12), calls=%async_computation.1 | async-start | bytes 4194304 | tf_op jit(solution)/shard_map/all_to_all | solution.py:215

commit v8 on v7

--- a/solution.py
+++ b/solution.py
@@ -164,11 +164,13 @@
             for g in range(unroll):
                 at_group = first + step * unroll + g
                 rows = [place[at_group * 8 + j] for j in range(8)]
-                for q in range(4):
-                    at = q // 2 * BACK_ROW + q % 2
-                    update[at_group, :, q * LANES : (q + 1) * LANES] = jnp.concatenate(
-                        [box[pl.ds(row + at, 1), :] for row in rows], axis=0
-                    )
+                for parity in range(2):
+                    halves = [box[pl.ds(row + parity * BACK_ROW, 2), :] for row in rows]
+                    for c in range(2):
+                        lane = (2 * parity + c) * LANES
+                        update[at_group, :, lane : lane + LANES] = jnp.concatenate(
+                            [half[c : c + 1] for half in halves], axis=0
+                        )
             return carry
 
         lax.fori_loop(0, size // unroll, group, 0)
@@ -227,7 +229,7 @@
     )(in_hbm(arrived), in_hbm(left_stat), in_hbm(right_stat), in_hbm(moment))
 
     update = call(
-        functools.partial(unpack_kernel, (24, 16, 8), 4), [SMEM, VMEM], HBM, jax.ShapeDtypeStruct(update_shape, F32),
+        functools.partial(unpack_kernel, (24, 16, 8), 8), [SMEM, VMEM], HBM, jax.ShapeDtypeStruct(update_shape, F32),
         [pltpu.VMEM(update_shape, F32), dma((3,))], 2 * grads.size, 16 * grads.size, 8,
     )(place, in_vmem(returned))
     return (update.reshape(grads.shape), left_new, right_new, moment_new)

time: 85.2 us -> 85.1 us (level)
  no operation moved by 1% of the time
where the time goes in v8:
time: 85.1 us; the launch traced here: 84.7 us
  blocking collectives  42.4 us (50%)
  waiting for transfers between devices  20.2 us (24%)
  Pallas kernels  16.8 us (20%)
  starting transfers between devices  4.55 us (5%)
    all_to_all x1, blocking collectives, exchange(): lax.all_to_all(rows, 'shard', split_axis=0, concat_axis=0, tiled=True)  42.4 us
    all_to_all x1, waiting for transfers between devices, shards(): lax.all_to_all(sent.reshape(back_shape), 'shard', split_axis=0, concat_ax...  20.2 us
    pallas_call x1, Pallas kernels, shards(): pl.pallas_call(functools.partial(stats_kernel, limit), grid=(SLOT_DEV,),...  10.3 us
    all_to_all x1, starting transfers between devices, shards(): lax.all_to_all(sent.reshape(back_shape), 'shard', split_axis=0, concat_ax...  4.55 us
    pallas_call x1, Pallas kernels, shards(): call(functools.partial(shape_kernel, limit, (2, 4)), [VMEM] * 4, HBM, plt...  2.61 us
    pallas_call x1, Pallas kernels, shards(): call(functools.partial(pack_kernel, 2), [HBM, HBM], [VMEM, VMEM], [pltpu....  2.19 us
  transfers between devices with their start and end apart: 1, of which 1 were waited for; matrix products, arithmetic and copies ran while one was open for 0% of the time, Pallas kernels for 12%

profile of v8, /device:TPU:1, one launch (start us, length us, event | category | flops | bytes accessed | tf_op | source)
XLA Modules:
  0.0 84.7 jit_solution(16806250064653016173)
XLA Ops:
  0.6 2.2 %shard_map.102 = (f32[4224,128]{1,0:T(8,128)S(1)}, s32[8,384]{1,0:T(8,128)S(1)}) custom-call(s32[1,384]{1,0:T(1,128)} %bitcast.14, f32[384,512]{1,0:T(8,128)} %grads_hbm.1), custom_call_target="tpu_custom_call" | custom-call | flops 805306368 | bytes 3145728 | tf_op jit(solution)/shard_map/pallas_call | solution.py:202
  2.8 0.0 copy-start.1
  2.8 0.0 copy-start.2
  2.9 0.0 copy-start.3
  2.9 42.4 %all_to_all.16 = f32[4224,1,128]{2,1,0:T(1,128)S(1)} all-to-all(f32[4224,1,128]{2,1,0:T(1,128)S(1)} %bitcast.11), channel_id=1, replica_groups=mesh['shard'=128] {'shard'}, dimensions={0} | all-to-all | bytes 4325376 | tf_op jit(solution)/shard_map/all_to_all | solution.py:186
  45.3 0.0 copy-start
  45.3 0.0 copy-done.1
  45.3 0.0 copy-done.2
  45.3 0.0 copy-done.3
  45.3 2.6 %shard_map.103 = f32[256,16,128]{2,1,0:T(8,128)} custom-call(f32[4224,128]{1,0:T(8,128)S(1)} %bitcast.8, bf16[8,256,256]{2,1,0:T(8,128)(2,1)S(1)} %copy-done.2, bf16[8,256,256]{2,1,0:T(8,128)(2,1)S(1)} %copy-done.3, f32[8,256,256]{2,1,0:T(8,128)S(1)} %copy-done.1), custom_call_target="tpu_custom_call" | custom-call | flops 536870912 | bytes 8388608 | tf_op jit(solution)/shard_map/pallas_call | solution.py:212
  47.9 0.0 copy-done
  47.9 4.6 %all-to-all-start.1 = ((f32[128,32,128]{2,1,0:T(8,128)}), f32[128,32,128]{2,1,0:T(8,128)S(1)}, u32[]{:S(2)}, u32[]{:S(2)}) async-start(f32[128,32,128]{2,1,0:T(8,128)} %bitcast.12), calls=%async_computation.1 | async-start | bytes 4194304 | tf_op jit(solution)/shard_map/all_to_all | solution.py:217
  52.5 10.3 %shard_map.105 = (f32[8,256,256]{2,1,0:T(8,128)}, f32[8,256,256]{2,1,0:T(8,128)}, f32[8,256,256]{2,1,0:T(8,128)}) custom-call(f32[4224,128]{1,0:T(8,128)} %bitcast.9, f32[8,256,256]{2,1,0:T(8,128)} %left.3, f32[8,256,256]{2,1,0:T(8,128)} %right.3, f32[8,256,256]{2,1,0:T(8,128)} %moment.3), custom_call_target="tpu_custom_call" | custom-call | flops 1610612736 | bytes 14680064 | tf_op jit(solution)/shard_map/pallas_call | solution.py:220
  62.8 20.2 %all-to-all-done.1 = f32[128,32,128]{2,1,0:T(8,128)S(1)} async-done(((f32[128,32,128]{2,1,0:T(8,128)}), f32[128,32,128]{2,1,0:T(8,128)S(1)}, u32[]{:S(2)}, u32[]{:S(2)}) %all-to-all-start.1) | async-done | bytes 2097184 | tf_op jit(solution)/shard_map/all_to_all | solution.py:217
  83.0 1.7 %shard_map.104 = f32[48,8,512]{2,1,0:T(8,128)} custom-call(s32[384]{0:T(512)S(1)} %slice_reduce_fusion.place, f32[4096,128]{1,0:T(8,128)S(1)} %bitcast.10), custom_call_target="tpu_custom_call" | custom-call | flops 393216 | bytes 3145728 | tf_op jit(solution)/shard_map/pallas_call | solution.py:231
  (1 shorter events, 0.0 us)
Async XLA Ops:
  2.8 42.5 %copy-start.1 = (f32[8,256,256]{2,1,0:T(8,128)S(1)}, f32[8,256,256]{2,1,0:T(8,128)}, u32[]{:S(2)}) copy-start(f32[8,256,256]{2,1,0:T(8,128)} %moment.3) | copy-start | bytes 6291460
  2.8 42.4 %copy-start.2 = (bf16[8,256,256]{2,1,0:T(8,128)(2,1)S(1)}, bf16[8,256,256]{2,1,0:T(8,128)(2,1)}, u32[]{:S(2)}) copy-start(bf16[8,256,256]{2,1,0:T(8,128)(2,1)} %left.2) | copy-start | bytes 3145732
  2.9 42.4 %copy-start.3 = (bf16[8,256,256]{2,1,0:T(8,128)(2,1)S(1)}, bf16[8,256,256]{2,1,0:T(8,128)(2,1)}, u32[]{:S(2)}) copy-start(bf16[8,256,256]{2,1,0:T(8,128)(2,1)} %right.2) | copy-start | bytes 3145732
  45.3 2.6 %copy-start = (f32[4224,1,128]{2,1,0:T(1,128)}, f32[4224,1,128]{2,1,0:T(1,128)S(1)}, u32[]{:S(2)}) copy-start(f32[4224,1,128]{2,1,0:T(1,128)S(1)} %all_to_all.16) | copy-start | bytes 6488068
  47.9 35.1 %all-to-all-start.1 = ((f32[128,32,128]{2,1,0:T(8,128)}), f32[128,32,128]{2,1,0:T(8,128)S(1)}, u32[]{:S(2)}, u32[]{:S(2)}) async-start(f32[128,32,128]{2,1,0:T(8,128)} %bitcast.12), calls=%async_computation.1 | async-start | bytes 4194304 | tf_op jit(solution)/shard_map/all_to_all | solution.py:217
